TPU v7x, 32 devices: a whole 2x2x4 slice. The times are simulated.
32 devices in a mesh: row: 8 (over y, x, core), col: 4 (over z).
Axes of the slice: x: 2, y: 2, z: 4, core: 2. Of those that a mesh axis runs over, the one named last changes fastest.
Arguments:
- features: bfloat16 [4096, 256], P(('row', 'col')), may hold values from -6 to 6
- tile_values: bfloat16 [8, 4, 8, 128, 128], P('row', 'col'), may hold values from -0.21875 to 0.21875
- tile_rows: int32 [8, 4, 8], P('row', 'col'), may hold values from 0 to 3, as said below
- tile_cols: int32 [8, 4, 8], P('row', 'col'), may hold values from 0 to 7
- tile_count: int32 [8, 4], P('row', 'col'), may hold values from 1 to 8, as said below
- weight: bfloat16 [256, 256], replicated, may hold values from -0.375 to 0.375
- out_grad: bfloat16 [4096, 256], P(('row', 'col')), may hold values from -6 to 6
Outputs:
- activated: bfloat16 [4096, 256], P(('row', 'col'))
- feature_grad: bfloat16 [4096, 256], P(('row', 'col'))
- weight_grad: float32 [256, 256], replicated
Inputs may be any that keep to these rules, and one draw needn't show every extreme that they name: Within one grid cell the pairs (tile_rows, tile_cols) of all 8 slots are distinct. `tile_count`: some grid cell has all 8 slots live.
All inputs are finite; a program needn't handle non-finite values.
Results may differ from a plain program's by a relative error of at most 0.023.
Values may be sent and summed in bfloat16 or wider, within the bound.
A program may use at most 64 MiB of HBM per device.

v0:
```python
import math

import jax
import jax.numpy as jnp
from jax import lax
from jax.sharding import PartitionSpec as P


def gelu_value(preact):
    return jax.nn.gelu(preact, approximate=True)


def gelu_backward(preact, upstream):
    _, pullback = jax.vjp(gelu_value, preact)
    return pullback(upstream)[0]


def combine_tiles(tiles, read_ids, write_ids, live_count, source_blocks, dest_tiles, transposed):
    slot_total = tiles.shape[0]
    tile_size = tiles.shape[1]
    feat_width = source_blocks.shape[2]
    group = math.gcd(slot_total, 32)
    slot_index = jnp.arange(group, dtype=jnp.int32)

    def one_group(group_index, running):
        offset = group_index * group
        live_part = slot_index + offset < live_count
        gathered = jnp.take(source_blocks, read_ids, axis=0)
        if transposed:
            products = jnp.einsum(
                "tab,taf->tbf", tiles, gathered, preferred_element_type=jnp.float32
            )
        else:
            products = jnp.einsum(
                "tab,tbf->taf", tiles, gathered, preferred_element_type=jnp.float32
            )
        products = jnp.where(live_part[:, None, None], products, jnp.float32(0.0))
        return running.at[write_ids].add(products)

    initial = jnp.zeros((dest_tiles, tile_size, feat_width), jnp.float32)
    groups_live = (live_count + (group - 1)) // group
    return lax.fori_loop(jnp.int32(0), groups_live, one_group, initial)


def body(features, tile_values, tile_rows, tile_cols, tile_count, weight, out_grad):
    tiles = tile_values[0, 0]
    row_ids = tile_rows[0, 0]
    col_ids = tile_cols[0, 0]
    live_count = tile_count[0, 0]
    tile_size = tiles.shape[1]
    node_rows, feat_width = features.shape
    grid_rows = lax.axis_size("row")
    grid_cols = lax.axis_size("col")
    row_tiles = grid_cols * node_rows // tile_size
    col_tiles = grid_rows * node_rows // tile_size
    projected = jnp.dot(features, weight, preferred_element_type=jnp.float32).astype(jnp.bfloat16)
    column_block = lax.all_gather(projected, "row", axis=0, tiled=True).reshape(
        col_tiles, tile_size, feat_width
    )
    partial_value = combine_tiles(
        tiles, col_ids, row_ids, live_count, column_block, row_tiles, False
    )
    partial_value = partial_value.reshape(row_tiles * tile_size, feat_width)
    own_rows = lax.psum_scatter(
        partial_value.astype(jnp.bfloat16), "col", scatter_dimension=0, tiled=True
    ).astype(jnp.float32)
    activated = gelu_value(own_rows).astype(jnp.bfloat16)
    cotangent = gelu_backward(own_rows, out_grad.astype(jnp.float32)).astype(jnp.bfloat16)
    cotangent_block = lax.all_gather(cotangent, "col", axis=0, tiled=True)
    row_blocks = cotangent_block.reshape(row_tiles, tile_size, feat_width)
    back_terms = combine_tiles(tiles, row_ids, col_ids, live_count, row_blocks, col_tiles, True)
    back_terms = back_terms.reshape(col_tiles * tile_size, feat_width)
    pulled = lax.psum_scatter(
        back_terms.astype(jnp.bfloat16), "row", scatter_dimension=0, tiled=True
    )
    weight_term = lax.dot_general(
        features, pulled, (((0,), (0,)), ((), ())), preferred_element_type=jnp.float32
    )
    total_nodes = node_rows * grid_rows * grid_cols
    weight_grad = lax.psum(weight_term, ("row", "col")) * total_nodes ** (-0.5)
    feature_grad = lax.dot_general(
        pulled, weight, (((1,), (1,)), ((), ())), preferred_element_type=jnp.float32
    ).astype(jnp.bfloat16)
    return (activated, feature_grad, weight_grad)


def solution(mesh):
    placed = (
        P(("row", "col"), None),
        P("row", "col", None, None, None),
        P("row", "col", None),
        P("row", "col", None),
        P("row", "col"),
        P(),
        P(("row", "col"), None),
    )
    return jax.shard_map(
        body,
        mesh=mesh,
        in_specs=placed,
        out_specs=(P(("row", "col"), None), P(("row", "col"), None), P()),
        check_vma=False,
    )
```

profile of v0, /device:TPU:0, one launch (start us, length us, event | category | flops | bytes accessed | tf_op | source)
XLA Modules:
  0.0 240.0 jit_solution(3267812917504471788)
XLA Ops:
  7.9 0.6 copy-done.5
  8.6 1.0 convolution_convert_fusion.1
  9.6 11.3 %all_gather.6 = bf16[1024,256]{1,0:T(8,128)(2,1)S(1)} all-gather(bf16[128,256]{1,0:T(8,128)(2,1)S(1)} %convolution_convert_fusion.1), channel_id=1, replica_groups=mesh['row'=8,'col'=4] {'row'}, dimensions={0}, use_global_device_ids=true | all-gather | bytes 589824 | tf_op jit(solution)/shard_map/all_gather | solution.py:57
  21.9 0.6 copy-done.4
  22.5 3.6 %while.24 = (s32[]{:T(128)}, f32[4,128,256]{2,1,0:T(8,128)S(1)}, s32[]{:T(128)}, s32[8]{0:T(128)S(1)}, s32[]{:T(128)}, /*index=5*/s32[8]{0:T(128)S(1)}, bf16[8,1...) while((s32[]{:T(128)}, f32[4,128,256]{2,1,0:T(8,128)S(1)}, ...), condition=%wide.region_2.3_spmd.clone, body=%wide.region_0.2_spmd.clone.sunk | while | flops 67895384 | bytes 7078169 | solution.py:42
  22.5 0.7 compare_and_fusion.4
  23.1 1.3 fusion.50
  24.8 1.3 scatter_fusion
  26.1 0.7 convert_element_type.31
  26.9 20.1 %reduce-scatter.3.cloned.1.call-done = bf16[128,256]{1,0:T(8,128)(2,1)} async-done(((bf16[512,256]{1,0:T(8,128)(2,1)}), bf16[128,256]{1,0:T(8,128)(2,1)}) %reduce-scatter.3.cloned.1.call-update) | async-done | bytes 65552 | tf_op jit(solution)/shard_map/reduce_scatter | solution.py:64
  47.0 1.6 fusion.22
  48.6 13.9 %all_gather.7 = bf16[512,256]{1,0:T(8,128)(2,1)S(1)} all-gather(bf16[128,256]{1,0:T(8,128)(2,1)S(1)} %get-tuple-element.252), channel_id=1, replica_groups=mesh['row'=8,'col'=4] {'col'}, dimensions={0}, use_global_device_ids=true | all-gather | bytes 327680 | tf_op jit(solution)/shard_map/all_gather | solution.py:69
  62.5 4.3 %while.25 = (s32[]{:T(128)}, f32[8,128,256]{2,1,0:T(8,128)S(1)}, s32[]{:T(128)}, s32[8]{0:T(128)S(1)}, s32[]{:T(128)}, /*index=5*/s32[8]{0:T(128)S(1)}, bf16[4,1...) while((s32[]{:T(128)}, f32[8,128,256]{2,1,0:T(8,128)S(1)}, ...), condition=%wide.region_6.7_spmd.clone, body=%wide.region_4.6_spmd.clone.sunk | while | flops 67896432 | bytes 8130969 | solution.py:42
  62.6 0.7 compare_and_fusion.5
  63.8 1.4 fusion.54
  65.6 1.3 scatter_fusion.1
  66.9 0.8 convert_element_type.37
  67.8 32.8 %reduce-scatter.5.cloned.1.call-done = bf16[128,256]{1,0:T(8,128)(2,1)} async-done(((bf16[1024,256]{1,0:T(8,128)(2,1)}), bf16[128,256]{1,0:T(8,128)(2,1)}) %reduce-scatter.5.cloned.1.call-update) | async-done | bytes 65552 | tf_op jit(solution)/shard_map/reduce_scatter | solution.py:73
  100.6 1.7 convolution_bitcast_fusion
  102.4 0.8 copy-done.2
  103.2 0.8 convolution_convert_fusion
  104.0 127.7 %all-reduce.2.cloned.1.call-done = f32[256,256]{0,1:T(8,128)} async-done(((f32[256,256]{0,1:T(8,128)}), f32[256,256]{0,1:T(8,128)}) %all-reduce.2.cloned.1.call-update) | async-done | bytes 262160 | tf_op jit(solution)/shard_map/psum | solution.py:80
  231.7 1.0 broadcast_multiply_fusion
  232.6 0.8 copy.18
  (27 shorter events, 2.4 us)
Async XLA Ops:
  7.2 1.4 copy-start
  7.2 39.8 %reduce-scatter.3.cloned.1.call-start = ((), (), s32[]{:S(2)}) async-start(), calls=%async_computation.2 | async-start | bytes 327680 | tf_op jit(solution)/shard_map/reduce_scatter | solution.py:64
  7.9 0.7 copy-start.5
  21.8 0.7 copy-start.4
  26.8 20.2 %copy-start.3 = (bf16[128,256]{1,0:T(8,128)(2,1)S(1)}, bf16[128,256]{1,0:T(8,128)(2,1)}, u32[]{:S(2)}) copy-start(bf16[128,256]{1,0:T(8,128)(2,1)} %param.17) | copy-start | bytes 196612
  26.9 73.7 %reduce-scatter.5.cloned.1.call-start = ((), (), s32[]{:S(2)}) async-start(), calls=%async_computation.3 | async-start | bytes 589824 | tf_op jit(solution)/shard_map/reduce_scatter | solution.py:73
  67.7 32.8 %copy-start.1 = (bf16[128,256]{1,0:T(8,128)(2,1)S(1)}, bf16[128,256]{1,0:T(8,128)(2,1)}, u32[]{:S(2)}) copy-start(bf16[128,256]{1,0:T(8,128)(2,1)} %param.11) | copy-start | bytes 196612
  67.8 163.9 %all-reduce.2.cloned.1.call-start = ((), (), s32[]{:S(2)}) async-start(), calls=%async_computation.4 | async-start | bytes 524288 | tf_op jit(solution)/shard_map/psum | solution.py:80
  102.3 0.8 copy-start.2
Sparse Core Ops, SparseCore 0:
  27.0 19.9 reduce-scatter.2
  67.9 32.6 reduce-scatter.4
  106.7 124.9 all-reduce.1
where the time goes:
time: 240 us
  waiting for transfers between devices  181 us (75%)
  blocking collectives  25.2 us (10%)
  between operations  14.5 us (6%)
  other arithmetic  8.09 us (3%)
  matrix products  6.24 us (3%)
  local copies, waits for them, and re-layouts  5.14 us (2%)
    psum x1, waiting for transfers between devices, body(): weight_grad = lax.psum(weight_term, ('row', 'col')) * total_nodes ** (-0.5)  128 us
    reduce_scatter x1, waiting for transfers between devices, body(): lax.psum_scatter(back_terms.astype(jnp.bfloat16), 'row', scatter_dimensio...  32.8 us
    reduce_scatter x1, waiting for transfers between devices, body(): lax.psum_scatter(partial_value.astype(jnp.bfloat16), 'col', scatter_dimen...  20.1 us
    all_gather x1, blocking collectives, body(): cotangent_block = lax.all_gather(cotangent, 'col', axis=0, tiled=True)  13.9 us
    all_gather x1, blocking collectives, body(): lax.all_gather(projected, 'row', axis=0, tiled=True)  11.3 us
  transfers between devices with their start and end apart: 3, of which 3 were waited for; matrix products, arithmetic and copies ran while one was open for 0% of the time, Pallas kernels for 0%

commit v1 on v0

v1 whole, which is shorter than its diff:
```python
import functools

import jax
import jax.numpy as jnp
from jax import lax
from jax.experimental import pallas as pl
from jax.experimental.pallas import tpu as pltpu
from jax.sharding import PartitionSpec as P

MESH = pl.DeviceIdType.MESH
F32 = jnp.float32
BF16 = jnp.bfloat16


def repeat(low, high, step):
    if high - low <= 8:
        for k in range(low, high):
            step(k)
    else:

        def once(k, carry):
            step(k)
            return carry

        lax.fori_loop(low, high, once, 0)


def block(index, size):
    if isinstance(index, int):
        return pl.ds(index * size, size)
    return pl.ds(pl.multiple_of(index * size, size), size)


def dot(a, b):
    return jnp.dot(a, b, preferred_element_type=F32)


def gelu_and_slope(v):
    scale = 0.7978845608028654
    square = v * v
    t = jnp.tanh(scale * (v + 0.044715 * v * square))
    half = 0.5 * (1.0 + t)
    slope = half + 0.5 * v * (1.0 - t * t) * scale * (1.0 + 3 * 0.044715 * square)
    return v * half, slope


def kernel(
    n_row, n_col,
    feat_in, tiles_in, rows_ref, cols_ref, count_ref, weight_in, upstream_in,
    act_out, fgrad_out, wgrad_out,
    feat_all, tiles, tiles_t, adj, adj_t, weight, weight_t, upstream,
    part_send, part_recv, cot_all, back_send, back_recv,
    w_send, w_recv, w_mid, w_all, act, fgrad, wgrad,
    in_sem, out_sem,
    feat_s, feat_r, part_s, part_r, cot_s, cot_r, back_s, back_r,
    w1_s, w1_r, w2_s, w2_r, w3_s, w3_r,
):
    i, j = lax.axis_index("row"), lax.axis_index("col")
    nodes, width = feat_in.shape
    slots, tile = tiles_in.shape[0], tiles_in.shape[1]
    row_tiles = n_col * nodes // tile
    col_tiles = n_row * nodes // tile
    half = width // 2
    piece = 2 * width // n_row

    def row_peer(k):
        return lax.rem(i + k, n_row)

    def col_peer(k):
        return lax.rem(j + k, n_col)

    def to_row(src, dst, send, recv, peer):
        return pltpu.make_async_remote_copy(
            src_ref=src, dst_ref=dst, send_sem=send, recv_sem=recv,
            device_id=(peer, j), device_id_type=MESH)

    def to_col(src, dst, send, recv, peer):
        return pltpu.make_async_remote_copy(
            src_ref=src, dst_ref=dst, send_sem=send, recv_sem=recv,
            device_id=(i, peer), device_id_type=MESH)

    loads = [
        pltpu.make_async_copy(feat_in, feat_all.at[block(i, nodes)], in_sem.at[0]),
        pltpu.make_async_copy(tiles_in, tiles.at[pl.ds(0, slots)], in_sem.at[1]),
        pltpu.make_async_copy(weight_in, weight, in_sem.at[2]),
        pltpu.make_async_copy(upstream_in, upstream, in_sem.at[3]),
    ]
    for load in loads:
        load.start()

    barrier = pltpu.get_barrier_semaphore()
    repeat(1, n_row, lambda k: pl.semaphore_signal(
        barrier, inc=1, device_id=(row_peer(k), j), device_id_type=MESH))
    repeat(1, n_col, lambda k: pl.semaphore_signal(
        barrier, inc=1, device_id=(i, col_peer(k)), device_id_type=MESH))
    pl.semaphore_wait(barrier, n_row + n_col - 2)

    def feat_copy(k, owner, peer):
        return to_row(feat_in, feat_all.at[block(owner, nodes)],
                      feat_s.at[k], feat_r.at[k], peer)

    repeat(1, n_row, lambda k: feat_copy(k, i, row_peer(k)).start())

    loads[1].wait()
    tiles[slots] = jnp.zeros((tile, tile), BF16)
    tiles_t[slots] = jnp.zeros((tile, tile), BF16)

    def flip(s):
        tiles_t[s] = tiles[s].T

    repeat(0, slots, flip)
    count = count_ref[0, 0]

    def place_row(r):
        def place(c):
            slot = jnp.int32(slots)
            for s in range(slots):
                hit = (rows_ref[0, 0, s] == r) & (cols_ref[0, 0, s] == c) & (s < count)
                slot = jnp.where(hit, jnp.int32(s), slot)
            adj[block(r, tile), block(c, tile)] = tiles[slot]
            adj_t[block(c, tile), block(r, tile)] = tiles_t[slot]

        repeat(0, col_tiles, place)

    repeat(0, row_tiles, place_row)
    loads[2].wait()
    loads[3].wait()
    weight_t[...] = weight[...].T

    loads[0].wait()
    repeat(1, n_row, lambda k: feat_copy(k, row_peer(n_row - k), row_peer(k)).wait_recv())

    def part_copy(k, owner, peer):
        return to_col(part_send.at[peer], part_recv.at[owner],
                      part_s.at[k], part_r.at[k], peer)

    def forward(k):
        peer = col_peer(k)
        part_send[peer] = dot(adj[block(peer, nodes), :], feat_all[...]).astype(BF16)
        part_copy(k, j, peer).start()

    repeat(1, n_col, forward)
    part_recv[j] = dot(adj[block(j, nodes), :], feat_all[...]).astype(BF16)
    repeat(1, n_col, lambda k: part_copy(k, col_peer(n_col - k), col_peer(k)).wait_recv())
    total = part_recv[0].astype(F32)
    for k in range(1, n_col):
        total = total + part_recv[k].astype(F32)
    aggregate = total.astype(BF16)
    value, slope = gelu_and_slope(dot(aggregate, weight[...]))
    cotangent = (upstream[...].astype(F32) * slope).astype(BF16)

    cot_all[block(j, nodes), :] = cotangent

    def cot_copy(k, owner, peer):
        return to_col(cot_all.at[block(owner, nodes)], cot_all.at[block(owner, nodes)],
                      cot_s.at[k], cot_r.at[k], peer)

    repeat(1, n_col, lambda k: cot_copy(k, j, col_peer(k)).start())
    act[...] = value.astype(BF16)
    act_store = pltpu.make_async_copy(act, act_out, out_sem.at[0])
    act_store.start()

    term = lax.dot_general(aggregate, cotangent, (((0,), (0,)), ((), ())),
                           preferred_element_type=F32)
    term = (term * (nodes * n_row * n_col) ** -0.5).astype(BF16)
    w_send[pl.ds(0, width), :] = term[:, :half]
    w_send[pl.ds(width, width), :] = term[:, half:]

    def w1_copy(k, owner, peer):
        return to_row(w_send.at[block(peer, piece)], w_recv.at[owner],
                      w1_s.at[k], w1_r.at[k], peer)

    repeat(1, n_row, lambda k: w1_copy(k, i, row_peer(k)).start())
    w_recv[i] = w_send[block(i, piece), :]

    repeat(1, n_col, lambda k: cot_copy(k, col_peer(n_col - k), col_peer(k)).wait_recv())

    def back_copy(k, owner, peer):
        return to_row(back_send.at[peer], back_recv.at[owner],
                      back_s.at[k], back_r.at[k], peer)

    def backward(k):
        peer = row_peer(k)
        back_send[peer] = dot(adj_t[block(peer, nodes), :], cot_all[...]).astype(BF16)
        back_copy(k, i, peer).start()

    repeat(1, n_row, backward)
    back_recv[i] = dot(adj_t[block(i, nodes), :], cot_all[...]).astype(BF16)

    repeat(1, n_row, lambda k: w1_copy(k, row_peer(n_row - k), row_peer(k)).wait_recv())
    summed = w_recv[0].astype(F32)
    for k in range(1, n_row):
        summed = summed + w_recv[k].astype(F32)
    w_mid[j] = summed.astype(BF16)

    def w2_copy(k, owner, peer):
        return to_col(w_mid.at[owner], w_mid.at[owner], w2_s.at[k], w2_r.at[k], peer)

    repeat(1, n_col, lambda k: w2_copy(k, j, col_peer(k)).start())
    repeat(1, n_col, lambda k: w2_copy(k, col_peer(n_col - k), col_peer(k)).wait_recv())
    summed = w_mid[0].astype(F32)
    for k in range(1, n_col):
        summed = summed + w_mid[k].astype(F32)
    w_all[block(i, piece), :] = summed.astype(BF16)

    def w3_copy(k, owner, peer):
        return to_row(w_all.at[block(owner, piece)], w_all.at[block(owner, piece)],
                      w3_s.at[k], w3_r.at[k], peer)

    repeat(1, n_row, lambda k: w3_copy(k, i, row_peer(k)).start())

    repeat(1, n_row, lambda k: back_copy(k, row_peer(n_row - k), row_peer(k)).wait_recv())
    pulled = back_recv[0].astype(F32)
    for k in range(1, n_row):
        pulled = pulled + back_recv[k].astype(F32)
    fgrad[...] = dot(pulled.astype(BF16), weight_t[...]).astype(BF16)
    fgrad_store = pltpu.make_async_copy(fgrad, fgrad_out, out_sem.at[1])
    fgrad_store.start()

    repeat(1, n_row, lambda k: w3_copy(k, row_peer(n_row - k), row_peer(k)).wait_recv())
    wgrad[:, pl.ds(0, half)] = w_all[pl.ds(0, width), :].astype(F32)
    wgrad[:, pl.ds(half, half)] = w_all[pl.ds(width, width), :].astype(F32)
    wgrad_store = pltpu.make_async_copy(wgrad, wgrad_out, out_sem.at[2])
    wgrad_store.start()

    def row_sent(k):
        peer = row_peer(k)
        feat_copy(k, i, peer).wait_send()
        w1_copy(k, i, peer).wait_send()
        back_copy(k, i, peer).wait_send()
        w3_copy(k, i, peer).wait_send()

    def col_sent(k):
        peer = col_peer(k)
        part_copy(k, j, peer).wait_send()
        cot_copy(k, j, peer).wait_send()
        w2_copy(k, j, peer).wait_send()

    repeat(1, n_row, row_sent)
    repeat(1, n_col, col_sent)
    act_store.wait()
    fgrad_store.wait()
    wgrad_store.wait()


def body(features, tile_values, tile_rows, tile_cols, tile_count, weight, out_grad):
    n_row, n_col = lax.axis_size("row"), lax.axis_size("col")
    nodes, width = features.shape
    slots, tile = tile_values.shape[2], tile_values.shape[3]
    tall, wide = n_col * nodes, n_row * nodes
    piece = 2 * width // n_row
    vmem, dma = pltpu.VMEM, pltpu.SemaphoreType.DMA
    anywhere = pl.BlockSpec(memory_space=pl.ANY)
    scalars = pl.BlockSpec(memory_space=pltpu.SMEM)
    return tuple(pl.pallas_call(
        functools.partial(kernel, n_row, n_col),
        out_shape=(
            jax.ShapeDtypeStruct((nodes, width), BF16),
            jax.ShapeDtypeStruct((nodes, width), BF16),
            jax.ShapeDtypeStruct((width, width), F32),
        ),
        in_specs=[anywhere, anywhere, scalars, scalars, scalars, anywhere, anywhere],
        out_specs=(anywhere, anywhere, anywhere),
        scratch_shapes=[
            vmem((wide, width), BF16),
            vmem((slots + 1, tile, tile), BF16),
            vmem((slots + 1, tile, tile), BF16),
            vmem((tall, wide), BF16),
            vmem((wide, tall), BF16),
            vmem((width, width), BF16),
            vmem((width, width), BF16),
            vmem((nodes, width), BF16),
            vmem((n_col, nodes, width), BF16),
            vmem((n_col, nodes, width), BF16),
            vmem((tall, width), BF16),
            vmem((n_row, nodes, width), BF16),
            vmem((n_row, nodes, width), BF16),
            vmem((2 * width, width // 2), BF16),
            vmem((n_row, piece, width // 2), BF16),
            vmem((n_col, piece, width // 2), BF16),
            vmem((2 * width, width // 2), BF16),
            vmem((nodes, width), BF16),
            vmem((nodes, width), BF16),
            vmem((width, width), F32),
            dma((4,)), dma((3,)),
            dma((n_row,)), dma((n_row,)), dma((n_col,)), dma((n_col,)),
            dma((n_col,)), dma((n_col,)), dma((n_row,)), dma((n_row,)),
            dma((n_row,)), dma((n_row,)), dma((n_col,)), dma((n_col,)),
            dma((n_row,)), dma((n_row,)),
        ],
        compiler_params=pltpu.CompilerParams(
            collective_id=0, has_side_effects=True, vmem_limit_bytes=56 * 1024 * 1024),
    )(features, tile_values[0, 0], tile_rows, tile_cols, tile_count, weight, out_grad))


def solution(mesh):
    placed = (
        P(("row", "col"), None),
        P("row", "col", None, None, None),
        P("row", "col", None),
        P("row", "col", None),
        P("row", "col"),
        P(),
        P(("row", "col"), None),
    )
    return jax.shard_map(
        body,
        mesh=mesh,
        in_specs=placed,
        out_specs=(P(("row", "col"), None), P(("row", "col"), None), P()),
        check_vma=False,
    )
```

time: 240 us -> 45.4 us (0.19)
  waiting for transfers between devices: 181 us -> 0 us
  Pallas kernels: 0 us -> 40.3 us
  blocking collectives: 25.2 us -> 0 us
  between operations: 14.5 us -> 1.3 us
  other arithmetic: 8.09 us -> 0 us
  matrix products: 6.24 us -> 0 us
    psum x1 -> x0, waiting for transfers between devices: 128 us -> none  [body(): weight_grad = lax.psum(weight_term, ('row', 'col')) * total_nodes ** (-0.5)]
    reduce_scatter x2 -> x0, waiting for transfers between devices: 52.8 us -> none  [the longest x1 32.8 us: body(): lax.psum_scatter(back_terms.astype(jnp.bfloat16), 'row', scatter_dimensio...]
    pallas_call x0 -> x1, Pallas kernels: none -> 40.3 us  [body(): pl.pallas_call(functools.partial(kernel, n_row, n_col), out_shape=(jax.Sh...]
    all_gather x2 -> x0, blocking collectives: 25.2 us -> none  [the longest x1 13.9 us: body(): cotangent_block = lax.all_gather(cotangent, 'col', axis=0, tiled=True)]
    dot_general x5 -> x0, matrix products: 6.24 us -> none  [the longest x1 1.75 us: body(): lax.dot_general(features, pulled, (((0,), (0,)), ((), ())), preferred_ele...]
    convert_element_type x3 -> x0, other arithmetic: 3.15 us -> none  [the longest x1 1.57 us: body(): gelu_backward(own_rows, out_grad.astype(jnp.float32)).astype(jnp.bfloat16)]
    scatter-add x2 -> x0, other arithmetic: 2.64 us -> none  [one_group(): return running.at[write_ids].add(products)]
  transfers between devices with their start and end apart: 3 -> 0, of which waited for: 3 -> 0; matrix products, arithmetic and copies ran while one was open for 0% -> 0% of each run, Pallas kernels for 0% -> 0%
where the time goes in v1:
time: 45.4 us; the launch traced here: 45.2 us
  Pallas kernels  40.3 us (89%)
  local copies, waits for them, and re-layouts  3.69 us (8%)
  between operations  1.3 us (3%)
    pallas_call x1, Pallas kernels, body(): pl.pallas_call(functools.partial(kernel, n_row, n_col), out_shape=(jax.Sh...  40.3 us
    unnamed x5, local copies, waits for them, and re-layouts  3.69 us

profile of v1, /device:TPU:0, one launch (start us, length us, event | category | flops | bytes accessed | tf_op | source)
XLA Modules:
  0.0 45.2 jit_solution(11325278617223551409)
XLA Ops:
  1.3 40.3 %shard_map.94 = (bf16[128,256]{1,0:T(8,128)(2,1)}, bf16[128,256]{1,0:T(8,128)(2,1)}, f32[256,256]{1,0:T(8,128)}) custom-call(bf16[128,256]{1,0:T(8,128)(2,1)} %feat_in.1, bf16[8,128,128]{2,1,0:T(8,128)(2,1)} %bitcast.1, s32[1,1,8]{2,1,0:T(1,128)} %rows_ref.1, s32[1,1,8]{2,1,0:T(1,128)} %cols_ref.1, s32[1,1]{1,0:T(1,128)S(6)} %copy.13.count_ref, ...), custom_call_target="tpu_custom_call" | custom-call | tf_op jit(solution)/shard_map/pallas_call | solution.py:255
  41.5 0.0 copy-start
  41.6 1.5 %copy.14 = bf16[128,256]{1,0:T(8,128)(2,1)} copy(bf16[128,256]{1,0:T(8,128)(2,1)} %get-tuple-element.6) | data formatting | bytes 131072
  43.1 1.5 %copy.15 = bf16[128,256]{1,0:T(8,128)(2,1)} copy(bf16[128,256]{1,0:T(8,128)(2,1)} %get-tuple-element.7) | data formatting | bytes 131072
  44.5 0.0 copy-done
  44.5 0.7 %copy.16 = f32[256,256]{1,0:T(8,128)} copy(f32[256,256]{1,0:T(8,128)S(1)} %copy-done) | data formatting | bytes 524288
Async XLA Ops:
  41.5 3.0 %copy-start = (f32[256,256]{1,0:T(8,128)S(1)}, f32[256,256]{1,0:T(8,128)}, u32[]{:S(2)}) copy-start(f32[256,256]{1,0:T(8,128)} %get-tuple-element.8) | copy-start | bytes 786436

commit v2 on v1

v2 whole, which is shorter than its diff:
```python
import functools

import jax
import jax.numpy as jnp
from jax import lax
from jax.experimental import pallas as pl
from jax.experimental.pallas import tpu as pltpu
from jax.sharding import PartitionSpec as P

MESH = pl.DeviceIdType.MESH
F32 = jnp.float32
BF16 = jnp.bfloat16


def repeat(low, high, step):
    if high - low <= 8:
        for k in range(low, high):
            step(k)
    else:

        def once(k, carry):
            step(k)
            return carry

        lax.fori_loop(low, high, once, 0)


def block(index, size):
    if isinstance(index, int):
        return pl.ds(index * size, size)
    return pl.ds(pl.multiple_of(index * size, size), size)


def partner(rank, k, size):
    assert size & (size - 1) == 0
    found, bit = 0, 1
    while bit < size:
        found = found + bit * ((rank // bit + k // bit) % 2)
        bit *= 2
    return found


def far_first(size, step):
    repeat(1, size, lambda m: step(size - m))


def dot(a, b):
    return jnp.dot(a, b, preferred_element_type=F32)


def gelu_and_slope(v):
    scale = 0.7978845608028654
    square = v * v
    t = jnp.tanh(scale * (v + 0.044715 * v * square))
    half = 0.5 * (1.0 + t)
    slope = half + 0.5 * v * (1.0 - t * t) * scale * (1.0 + 3 * 0.044715 * square)
    return v * half, slope


PARTS = 1


def kernel(
    n_row, n_col,
    feat_in, tiles_in, rows_ref, cols_ref, count_ref, weight_in, upstream_in,
    act_out, fgrad_out, wgrad_out,
    feat_all, tiles, tiles_t, adj, adj_t, weight, weight_t, upstream,
    part_send, part_recv, cot_all, sib_send, sib_recv, back_send, back_recv,
    w_send, w_recv, w_mid, w_all, act, fgrad, wgrad,
    in_sem, out_sem, sib_s, sib_r,
    feat_s, feat_r, fwd_s, fwd_r, part_s, part_r, cot_s, cot_r,
    pair_s, pair_r, back_s, back_r, w1_s, w1_r, w2_s, w2_r, w3_s, w3_r,
):
    i, j = lax.axis_index("row"), lax.axis_index("col")
    chip, core = i // 2, i % 2
    n_chip = n_row // 2
    sibling = 2 * chip + 1 - core
    nodes, width = feat_in.shape
    slots, tile = tiles_in.shape[0], tiles_in.shape[1]
    row_tiles = n_col * nodes // tile
    col_tiles = n_row * nodes // tile
    half = width // 2
    piece = 2 * width // n_row
    lanes = width // PARTS

    def to_row(src, dst, send, recv, peer):
        return pltpu.make_async_remote_copy(
            src_ref=src, dst_ref=dst, send_sem=send, recv_sem=recv,
            device_id=(peer, j), device_id_type=MESH)

    def to_col(src, dst, send, recv, peer):
        return pltpu.make_async_remote_copy(
            src_ref=src, dst_ref=dst, send_sem=send, recv_sem=recv,
            device_id=(i, peer), device_id_type=MESH)

    def row_peer(k):
        return partner(i, k, n_row)

    def col_peer(k):
        return partner(j, k, n_col)

    def mate(k):
        return 2 * partner(chip, k, n_chip) + core

    def strip(h):
        return pl.ds(h * lanes, lanes)

    loads = [
        pltpu.make_async_copy(tiles_in, tiles.at[pl.ds(0, slots)], in_sem.at[0]),
        pltpu.make_async_copy(weight_in, weight, in_sem.at[1]),
        pltpu.make_async_copy(upstream_in, upstream, in_sem.at[2]),
    ] + [
        pltpu.make_async_copy(feat_in.at[:, strip(h)], feat_all.at[h, block(i, nodes)],
                              in_sem.at[3 + h])
        for h in range(PARTS)
    ]
    for load in loads:
        load.start()

    barrier = pltpu.get_barrier_semaphore()
    repeat(1, n_row, lambda k: pl.semaphore_signal(
        barrier, inc=1, device_id=(row_peer(k), j), device_id_type=MESH))
    repeat(1, n_col, lambda k: pl.semaphore_signal(
        barrier, inc=1, device_id=(i, col_peer(k)), device_id_type=MESH))
    pl.semaphore_wait(barrier, n_row + n_col - 2)

    def feat_copy(h, k, owner):
        return to_row(feat_in.at[:, strip(h)], feat_all.at[h, block(owner, nodes)],
                      feat_s.at[h, k], feat_r.at[h, k], mate(k))

    def sib_copy(h, owner):
        return to_row(feat_in.at[:, strip(h)], feat_all.at[h, block(owner, nodes)],
                      sib_s.at[h], sib_r.at[h], sibling)

    def pass_copy(h, k, owner):
        place = feat_all.at[h, block(owner, nodes)]
        return to_row(place, place, fwd_s.at[h, k], fwd_r.at[h, k], sibling)

    for h in range(PARTS):
        far_first(n_chip, lambda k: feat_copy(h, k, i).start())
        sib_copy(h, i).start()

    loads[0].wait()
    tiles[slots] = jnp.zeros((tile, tile), BF16)
    tiles_t[slots] = jnp.zeros((tile, tile), BF16)

    def flip(s):
        tiles_t[s] = tiles[s].T

    repeat(0, slots, flip)
    count = count_ref[0, 0]

    def place_row(r):
        def place(c):
            slot = jnp.int32(slots)
            for s in range(slots):
                hit = (rows_ref[0, 0, s] == r) & (cols_ref[0, 0, s] == c) & (s < count)
                slot = jnp.where(hit, jnp.int32(s), slot)
            adj[block(r, tile), block(c, tile)] = tiles[slot]
            adj_t[block(c, tile), block(r, tile)] = tiles_t[slot]

        repeat(0, col_tiles, place)

    repeat(0, row_tiles, place_row)
    for load in loads[1:]:
        load.wait()
    weight_t[...] = weight[...].T

    def part_copy(h, k):
        return to_col(part_send.at[h, k], part_recv.at[h, k],
                      part_s.at[h, k], part_r.at[h, k], col_peer(k))

    for h in range(PARTS):

        def pass_on(k):
            feat_copy(h, k, mate(k)).wait_recv()
            pass_copy(h, k, mate(k)).start()

        far_first(n_chip, pass_on)
        sib_copy(h, sibling).wait_recv()
        far_first(n_chip, lambda k: pass_copy(h, k, mate(k) + sibling - i).wait_recv())

        def forward(k):
            rows = block(col_peer(k), nodes)
            part_send[h, k] = dot(adj[rows, :], feat_all[h]).astype(BF16)
            part_copy(h, k).start()

        far_first(n_col, forward)
        part_recv[h, 0] = dot(adj[block(j, nodes), :], feat_all[h]).astype(BF16)

    gathered = []
    preact = jnp.zeros((nodes, width), F32)
    for h in range(PARTS):
        far_first(n_col, lambda k: part_copy(h, k).wait_recv())
        total = part_recv[h, 0].astype(F32)
        for k in range(1, n_col):
            total = total + part_recv[h, k].astype(F32)
        gathered.append(total.astype(BF16))
        preact = preact + dot(gathered[h], weight[strip(h), :])
    aggregate = jnp.concatenate(gathered, axis=1)
    value, slope = gelu_and_slope(preact)
    cotangent = (upstream[...].astype(F32) * slope).astype(BF16)

    def cot_copy(h, k, owner):
        place = cot_all.at[h, block(owner, nodes)]
        return to_col(place, place, cot_s.at[h, k], cot_r.at[h, k], col_peer(k))

    for h in range(PARTS):
        cot_all[h, block(j, nodes), :] = cotangent[:, h * lanes:(h + 1) * lanes]
        far_first(n_col, lambda k: cot_copy(h, k, j).start())
    act[...] = value.astype(BF16)
    act_store = pltpu.make_async_copy(act, act_out, out_sem.at[0])
    act_store.start()

    term = lax.dot_general(aggregate, cotangent, (((0,), (0,)), ((), ())),
                           preferred_element_type=F32)
    term = (term * (nodes * n_row * n_col) ** -0.5).astype(BF16)
    w_send[pl.ds(0, width), :] = term[:, :half]
    w_send[pl.ds(width, width), :] = term[:, half:]

    def w1_copy(k):
        return to_row(w_send.at[block(row_peer(k), piece)], w_recv.at[k],
                      w1_s.at[k], w1_r.at[k], row_peer(k))

    far_first(n_row, lambda k: w1_copy(k).start())
    w_recv[0] = w_send[block(i, piece), :]

    def pair_copy(h, k):
        return to_row(sib_send.at[h, k], sib_recv.at[h, k],
                      pair_s.at[h, k], pair_r.at[h, k], sibling)

    def back_copy(h, k):
        return to_row(back_send.at[h, k], back_recv.at[h, k],
                      back_s.at[h, k], back_r.at[h, k], mate(k))

    def back_dot(h, owner):
        return dot(adj_t[block(owner, nodes), :], cot_all[h])

    own = []
    for h in range(PARTS):
        far_first(n_col, lambda k: cot_copy(h, k, col_peer(k)).wait_recv())

        def to_sibling(k):
            sib_send[h, k] = back_dot(h, mate(k) + sibling - i).astype(BF16)
            pair_copy(h, k).start()

        def to_owner(k):
            mine = back_dot(h, mate(k))
            pair_copy(h, k).wait_recv()
            back_send[h, k] = (mine + sib_recv[h, k].astype(F32)).astype(BF16)
            back_copy(h, k).start()

        far_first(n_chip, to_sibling)
        to_sibling(0)
        far_first(n_chip, to_owner)
        mine = back_dot(h, i)
        pair_copy(h, 0).wait_recv()
        own.append(mine + sib_recv[h, 0].astype(F32))

    far_first(n_row, lambda k: w1_copy(k).wait_recv())
    summed = w_recv[0].astype(F32)
    for k in range(1, n_row):
        summed = summed + w_recv[k].astype(F32)
    w_mid[j] = summed.astype(BF16)

    def w2_copy(k, owner):
        return to_col(w_mid.at[owner], w_mid.at[owner], w2_s.at[k], w2_r.at[k], col_peer(k))

    far_first(n_col, lambda k: w2_copy(k, j).start())
    far_first(n_col, lambda k: w2_copy(k, col_peer(k)).wait_recv())
    summed = w_mid[0].astype(F32)
    for k in range(1, n_col):
        summed = summed + w_mid[k].astype(F32)
    w_all[block(i, piece), :] = summed.astype(BF16)

    def w3_copy(k, owner):
        place = w_all.at[block(owner, piece)]
        return to_row(place, place, w3_s.at[k], w3_r.at[k], row_peer(k))

    far_first(n_row, lambda k: w3_copy(k, i).start())

    grad = jnp.zeros((nodes, width), F32)
    for h in range(PARTS):
        far_first(n_chip, lambda k: back_copy(h, k).wait_recv())
        pulled = own[h]
        for k in range(1, n_chip):
            pulled = pulled + back_recv[h, k].astype(F32)
        grad = grad + dot(pulled.astype(BF16), weight_t[strip(h), :])
    fgrad[...] = grad.astype(BF16)
    fgrad_store = pltpu.make_async_copy(fgrad, fgrad_out, out_sem.at[1])
    fgrad_store.start()

    far_first(n_row, lambda k: w3_copy(k, row_peer(k)).wait_recv())
    wgrad[:, pl.ds(0, half)] = w_all[pl.ds(0, width), :].astype(F32)
    wgrad[:, pl.ds(half, half)] = w_all[pl.ds(width, width), :].astype(F32)
    wgrad_store = pltpu.make_async_copy(wgrad, wgrad_out, out_sem.at[2])
    wgrad_store.start()

    def row_sent(k):
        w1_copy(k).wait_send()
        w3_copy(k, i).wait_send()

    repeat(1, n_row, row_sent)
    repeat(1, n_col, lambda k: w2_copy(k, j).wait_send())
    for h in range(PARTS):

        def chip_sent(k):
            feat_copy(h, k, i).wait_send()
            pass_copy(h, k, mate(k)).wait_send()
            pair_copy(h, k).wait_send()
            back_copy(h, k).wait_send()

        def col_sent(k):
            part_copy(h, k).wait_send()
            cot_copy(h, k, j).wait_send()

        sib_copy(h, i).wait_send()
        pair_copy(h, 0).wait_send()
        repeat(1, n_chip, chip_sent)
        repeat(1, n_col, col_sent)
    act_store.wait()
    fgrad_store.wait()
    wgrad_store.wait()


def hand_over(*refs):
    sources, results, sems = refs[:3], refs[3:6], refs[6]
    copies = [
        pltpu.make_async_copy(source, result, sems.at[n])
        for n, (source, result) in enumerate(zip(sources, results))
    ]
    for copy in copies:
        copy.start()
    for copy in copies:
        copy.wait()


def body(features, tile_values, tile_rows, tile_cols, tile_count, weight, out_grad):
    n_row, n_col = lax.axis_size("row"), lax.axis_size("col")
    n_chip = n_row // 2
    nodes, width = features.shape
    slots, tile = tile_values.shape[2], tile_values.shape[3]
    tall, wide = n_col * nodes, n_row * nodes
    piece = 2 * width // n_row
    lanes = width // PARTS
    vmem, dma = pltpu.VMEM, pltpu.SemaphoreType.DMA
    anywhere = pl.BlockSpec(memory_space=pl.ANY)
    scalars = pl.BlockSpec(memory_space=pltpu.SMEM)
    shapes = (
        jax.ShapeDtypeStruct((nodes, width), BF16),
        jax.ShapeDtypeStruct((nodes, width), BF16),
        jax.ShapeDtypeStruct((width, width), F32),
    )
    results = pl.pallas_call(
        functools.partial(kernel, n_row, n_col),
        out_shape=shapes,
        in_specs=[anywhere, anywhere, scalars, scalars, scalars, anywhere, anywhere],
        out_specs=(anywhere, anywhere, anywhere),
        scratch_shapes=[
            vmem((PARTS, wide, lanes), BF16),
            vmem((slots + 1, tile, tile), BF16),
            vmem((slots + 1, tile, tile), BF16),
            vmem((tall, wide), BF16),
            vmem((wide, tall), BF16),
            vmem((width, width), BF16),
            vmem((width, width), BF16),
            vmem((nodes, width), BF16),
            vmem((PARTS, n_col, nodes, lanes), BF16),
            vmem((PARTS, n_col, nodes, lanes), BF16),
            vmem((PARTS, tall, lanes), BF16),
            vmem((PARTS, n_chip, nodes, lanes), BF16),
            vmem((PARTS, n_chip, nodes, lanes), BF16),
            vmem((PARTS, n_chip, nodes, lanes), BF16),
            vmem((PARTS, n_chip, nodes, lanes), BF16),
            vmem((2 * width, width // 2), BF16),
            vmem((n_row, piece, width // 2), BF16),
            vmem((n_col, piece, width // 2), BF16),
            vmem((2 * width, width // 2), BF16),
            vmem((nodes, width), BF16),
            vmem((nodes, width), BF16),
            vmem((width, width), F32),
            dma((3 + PARTS,)), dma((3,)), dma((PARTS,)), dma((PARTS,)),
        ]
        + [dma((PARTS, n_chip))] * 4
        + [dma((PARTS, n_col))] * 4
        + [dma((PARTS, n_chip))] * 4
        + [dma((n_row,))] * 2 + [dma((n_col,))] * 2 + [dma((n_row,))] * 2,
        compiler_params=pltpu.CompilerParams(
            collective_id=0, has_side_effects=True, vmem_limit_bytes=56 * 1024 * 1024),
    )(features, tile_values[0, 0], tile_rows, tile_cols, tile_count, weight, out_grad)
    return tuple(pl.pallas_call(
        hand_over,
        out_shape=shapes,
        in_specs=[anywhere] * 3,
        out_specs=(anywhere,) * 3,
        scratch_shapes=[dma((3,))],
    )(*results))


def solution(mesh):
    placed = (
        P(("row", "col"), None),
        P("row", "col", None, None, None),
        P("row", "col", None),
        P("row", "col", None),
        P("row", "col"),
        P(),
        P(("row", "col"), None),
    )
    return jax.shard_map(
        body,
        mesh=mesh,
        in_specs=placed,
        out_specs=(P(("row", "col"), None), P(("row", "col"), None), P()),
        check_vma=False,
    )
```

time: 45.4 us -> 52 us (1.15)
  Pallas kernels: 40.3 us -> 50.5 us
  local copies, waits for them, and re-layouts: 3.69 us -> 0 us
    pallas_call x1 -> x2, Pallas kernels: 40.3 us -> 50.5 us  [the longest x1 37.5 us: body(): pl.pallas_call(functools.partial(kernel, n_row, n_col), out_shape=shapes,...]
    unnamed x5 -> x0, local copies, waits for them, and re-layouts: 3.69 us -> none
where the time goes in v2:
time: 52 us; the launch traced here: 51.8 us
  Pallas kernels  50.5 us (97%)
  between operations  1.29 us (2%)
    pallas_call x1, Pallas kernels, body(): pl.pallas_call(functools.partial(kernel, n_row, n_col), out_shape=shapes,...  37.5 us
    pallas_call x1, Pallas kernels, body(): pl.pallas_call(hand_over, out_shape=shapes, in_specs=[anywhere] * 3, out_...  13 us

profile of v2, /device:TPU:0, one launch (start us, length us, event | category | flops | bytes accessed | tf_op | source)
XLA Modules:
  0.0 51.8 jit_solution(13444180378200667722)
XLA Ops:
  1.3 37.5 %shard_map.94 = (bf16[128,256]{1,0:T(8,128)(2,1)}, bf16[128,256]{1,0:T(8,128)(2,1)}, f32[256,256]{1,0:T(8,128)}) custom-call(bf16[128,256]{1,0:T(8,128)(2,1)} %feat_in.1, bf16[8,128,128]{2,1,0:T(8,128)(2,1)} %bitcast.1, s32[1,1,8]{2,1,0:T(1,128)} %rows_ref.1, s32[1,1,8]{2,1,0:T(1,128)} %cols_ref.1, s32[1,1]{1,0:T(1,128)S(6)} %copy.10.count_ref, ...), custom_call_target="tpu_custom_call" | custom-call | tf_op jit(solution)/shard_map/pallas_call | solution.py:354
  38.7 13.0 %shard_map.95 = (bf16[128,256]{1,0:T(8,128)(2,1)}, bf16[128,256]{1,0:T(8,128)(2,1)}, f32[256,256]{1,0:T(8,128)}) custom-call(bf16[128,256]{1,0:T(8,128)(2,1)} %get-tuple-element.6.refs_0_, bf16[128,256]{1,0:T(8,128)(2,1)} %get-tuple-element.7.refs_1_, f32[256,256]{1,0:T(8,128)} %get-tuple-element.8.refs_2_), custom_call_target="tpu_custom_call" | custom-call | tf_op jit(solution)/shard_map/pallas_call | solution.py:391

commit v3 on v2

--- a/solution.py
+++ b/solution.py
@@ -63,11 +63,11 @@
 def kernel(
     n_row, n_col,
     feat_in, tiles_in, rows_ref, cols_ref, count_ref, weight_in, upstream_in,
-    act_out, fgrad_out, wgrad_out,
+    act, fgrad, wgrad,
     feat_all, tiles, tiles_t, adj, adj_t, weight, weight_t, upstream,
     part_send, part_recv, cot_all, sib_send, sib_recv, back_send, back_recv,
-    w_send, w_recv, w_mid, w_all, act, fgrad, wgrad,
-    in_sem, out_sem, sib_s, sib_r,
+    w_send, w_recv, w_mid, w_all,
+    in_sem, sib_s, sib_r,
     feat_s, feat_r, fwd_s, fwd_r, part_s, part_r, cot_s, cot_r,
     pair_s, pair_r, back_s, back_r, w1_s, w1_r, w2_s, w2_r, w3_s, w3_r,
 ):
@@ -209,8 +209,6 @@
         cot_all[h, block(j, nodes), :] = cotangent[:, h * lanes:(h + 1) * lanes]
         far_first(n_col, lambda k: cot_copy(h, k, j).start())
     act[...] = value.astype(BF16)
-    act_store = pltpu.make_async_copy(act, act_out, out_sem.at[0])
-    act_store.start()
 
     term = lax.dot_general(aggregate, cotangent, (((0,), (0,)), ((), ())),
                            preferred_element_type=F32)
@@ -287,14 +285,10 @@
             pulled = pulled + back_recv[h, k].astype(F32)
         grad = grad + dot(pulled.astype(BF16), weight_t[strip(h), :])
     fgrad[...] = grad.astype(BF16)
-    fgrad_store = pltpu.make_async_copy(fgrad, fgrad_out, out_sem.at[1])
-    fgrad_store.start()
 
     far_first(n_row, lambda k: w3_copy(k, row_peer(k)).wait_recv())
     wgrad[:, pl.ds(0, half)] = w_all[pl.ds(0, width), :].astype(F32)
     wgrad[:, pl.ds(half, half)] = w_all[pl.ds(width, width), :].astype(F32)
-    wgrad_store = pltpu.make_async_copy(wgrad, wgrad_out, out_sem.at[2])
-    wgrad_store.start()
 
     def row_sent(k):
         w1_copy(k).wait_send()
@@ -318,9 +312,6 @@
         pair_copy(h, 0).wait_send()
         repeat(1, n_chip, chip_sent)
         repeat(1, n_col, col_sent)
-    act_store.wait()
-    fgrad_store.wait()
-    wgrad_store.wait()
 
 
 def hand_over(*refs):
@@ -345,6 +336,7 @@
     lanes = width // PARTS
     vmem, dma = pltpu.VMEM, pltpu.SemaphoreType.DMA
     anywhere = pl.BlockSpec(memory_space=pl.ANY)
+    in_vmem = pl.BlockSpec(memory_space=pltpu.VMEM)
     scalars = pl.BlockSpec(memory_space=pltpu.SMEM)
     shapes = (
         jax.ShapeDtypeStruct((nodes, width), BF16),
@@ -353,9 +345,9 @@
     )
     results = pl.pallas_call(
         functools.partial(kernel, n_row, n_col),
-        out_shape=shapes,
+        out_shape=tuple(pltpu.VMEM(s.shape, s.dtype) for s in shapes),
         in_specs=[anywhere, anywhere, scalars, scalars, scalars, anywhere, anywhere],
-        out_specs=(anywhere, anywhere, anywhere),
+        out_specs=(in_vmem,) * 3,
         scratch_shapes=[
             vmem((PARTS, wide, lanes), BF16),
             vmem((slots + 1, tile, tile), BF16),
@@ -376,10 +368,7 @@
             vmem((n_row, piece, width // 2), BF16),
             vmem((n_col, piece, width // 2), BF16),
             vmem((2 * width, width // 2), BF16),
-            vmem((nodes, width), BF16),
-            vmem((nodes, width), BF16),
-            vmem((width, width), F32),
-            dma((3 + PARTS,)), dma((3,)), dma((PARTS,)), dma((PARTS,)),
+            dma((3 + PARTS,)), dma((PARTS,)), dma((PARTS,)),
         ]
         + [dma((PARTS, n_chip))] * 4
         + [dma((PARTS, n_col))] * 4
@@ -391,7 +380,7 @@
     return tuple(pl.pallas_call(
         hand_over,
         out_shape=shapes,
-        in_specs=[anywhere] * 3,
+        in_specs=[in_vmem] * 3,
         out_specs=(anywhere,) * 3,
         scratch_shapes=[dma((3,))],
     )(*results))

time: 52 us -> 42 us (0.81)
  Pallas kernels: 50.5 us -> 38.6 us
  local copies, waits for them, and re-layouts: 0 us -> 1.93 us
    pallas_call x2, Pallas kernels: 50.5 us -> 38.6 us  [the longest x1 36.8 us: body(): pl.pallas_call(functools.partial(kernel, n_row, n_col), out_shape=tuple((...]
    unnamed x0 -> x6, local copies, waits for them, and re-layouts: none -> 1.93 us
where the time goes in v3:
time: 42 us; the launch traced here: 41.8 us
  Pallas kernels  38.6 us (92%)
  local copies, waits for them, and re-layouts  1.93 us (5%)
  between operations  1.3 us (3%)
    pallas_call x1, Pallas kernels, body(): pl.pallas_call(functools.partial(kernel, n_row, n_col), out_shape=tuple((...  36.8 us
    unnamed x6, local copies, waits for them, and re-layouts  1.93 us
    pallas_call x1, Pallas kernels, body(): pl.pallas_call(hand_over, out_shape=shapes, in_specs=[in_vmem] * 3, out_s...  1.8 us

profile of v3, /device:TPU:0, one launch (start us, length us, event | category | flops | bytes accessed | tf_op | source)
XLA Modules:
  0.0 41.8 jit_solution(13621987727868791279)
XLA Ops:
  1.3 36.8 %shard_map.94 = (bf16[128,256]{1,0:T(8,128)(2,1)S(1)}, bf16[128,256]{1,0:T(8,128)(2,1)S(1)}, f32[256,256]{1,0:T(8,128)S(1)}) custom-call(bf16[128,256]{1,0:T(8,128)(2,1)} %feat_in.1, bf16[8,128,128]{2,1,0:T(8,128)(2,1)} %bitcast.1, s32[1,1,8]{2,1,0:T(1,128)} %rows_ref.1, s32[1,1,8]{2,1,0:T(1,128)} %cols_ref.1, s32[1,1]{1,0:T(1,128)S(6)} %copy.10.count_ref, ...), custom_call_target="tpu_custom_call" | custom-call | tf_op jit(solution)/shard_map/pallas_call | solution.py:346
  38.1 0.0 copy-start
  38.1 0.7 %copy-done = f32[256,256]{1,0:T(8,128)} copy-done((f32[256,256]{1,0:T(8,128)}, f32[256,256]{1,0:T(8,128)S(1)}, u32[]{:S(2)}) %copy-start) | copy-done | bytes 262168
  38.8 0.0 copy-start.1
  38.8 0.6 %copy-done.1 = bf16[128,256]{1,0:T(8,128)(2,1)} copy-done((bf16[128,256]{1,0:T(8,128)(2,1)}, bf16[128,256]{1,0:T(8,128)(2,1)S(1)}, u32[]{:S(2)}) %copy-start.1) | copy-done | bytes 65560
  39.4 0.0 copy-start.2
  39.4 0.6 %copy-done.2 = bf16[128,256]{1,0:T(8,128)(2,1)} copy-done((bf16[128,256]{1,0:T(8,128)(2,1)}, bf16[128,256]{1,0:T(8,128)(2,1)S(1)}, u32[]{:S(2)}) %copy-start.2) | copy-done | bytes 65560
  40.0 1.8 %shard_map.95 = (bf16[128,256]{1,0:T(8,128)(2,1)}, bf16[128,256]{1,0:T(8,128)(2,1)}, f32[256,256]{1,0:T(8,128)}) custom-call(bf16[128,256]{1,0:T(8,128)(2,1)} %copy-done.1, bf16[128,256]{1,0:T(8,128)(2,1)} %copy-done.2, f32[256,256]{1,0:T(8,128)} %copy-done), custom_call_target="tpu_custom_call" | custom-call | tf_op jit(solution)/shard_map/pallas_call | solution.py:380
Async XLA Ops:
  38.1 0.7 %copy-start = (f32[256,256]{1,0:T(8,128)}, f32[256,256]{1,0:T(8,128)S(1)}, u32[]{:S(2)}) copy-start(f32[256,256]{1,0:T(8,128)S(1)} %get-tuple-element.8.refs_2_) | copy-start | bytes 786436
  38.8 0.6 %copy-start.1 = (bf16[128,256]{1,0:T(8,128)(2,1)}, bf16[128,256]{1,0:T(8,128)(2,1)S(1)}, u32[]{:S(2)}) copy-start(bf16[128,256]{1,0:T(8,128)(2,1)S(1)} %get-tuple-element.6.refs_0_) | copy-start | bytes 196612
  39.4 0.6 %copy-start.2 = (bf16[128,256]{1,0:T(8,128)(2,1)}, bf16[128,256]{1,0:T(8,128)(2,1)S(1)}, u32[]{:S(2)}) copy-start(bf16[128,256]{1,0:T(8,128)(2,1)S(1)} %get-tuple-element.7.refs_1_) | copy-start | bytes 196612

commit v4 on v3

--- a/solution.py
+++ b/solution.py
@@ -57,7 +57,7 @@
     return v * half, slope
 
 
-PARTS = 1
+PARTS = 2
 
 
 def kernel(

time: 42 us -> 41.5 us (0.988)
  Pallas kernels: 38.6 us -> 38.1 us
    pallas_call x1, Pallas kernels: 36.8 us -> 36.3 us  [body(): pl.pallas_call(functools.partial(kernel, n_row, n_col), out_shape=tuple((...]
where the time goes in v4:
time: 41.5 us; the launch traced here: 41.3 us
  Pallas kernels  38.1 us (92%)
  local copies, waits for them, and re-layouts  1.93 us (5%)
  between operations  1.3 us (3%)
    pallas_call x1, Pallas kernels, body(): pl.pallas_call(functools.partial(kernel, n_row, n_col), out_shape=tuple((...  36.3 us
    unnamed x6, local copies, waits for them, and re-layouts  1.93 us
    pallas_call x1, Pallas kernels, body(): pl.pallas_call(hand_over, out_shape=shapes, in_specs=[in_vmem] * 3, out_s...  1.8 us

profile of v4, /device:TPU:0, one launch (start us, length us, event | category | flops | bytes accessed | tf_op | source)
XLA Modules:
  0.0 41.3 jit_solution(6236424776474213202)
XLA Ops:
  1.3 36.3 %shard_map.94 = (bf16[128,256]{1,0:T(8,128)(2,1)S(1)}, bf16[128,256]{1,0:T(8,128)(2,1)S(1)}, f32[256,256]{1,0:T(8,128)S(1)}) custom-call(bf16[128,256]{1,0:T(8,128)(2,1)} %feat_in.1, bf16[8,128,128]{2,1,0:T(8,128)(2,1)} %bitcast.1, s32[1,1,8]{2,1,0:T(1,128)} %rows_ref.1, s32[1,1,8]{2,1,0:T(1,128)} %cols_ref.1, s32[1,1]{1,0:T(1,128)S(6)} %copy.10.count_ref, ...), custom_call_target="tpu_custom_call" | custom-call | tf_op jit(solution)/shard_map/pallas_call | solution.py:346
  37.6 0.0 copy-start
  37.6 0.7 %copy-done = f32[256,256]{1,0:T(8,128)} copy-done((f32[256,256]{1,0:T(8,128)}, f32[256,256]{1,0:T(8,128)S(1)}, u32[]{:S(2)}) %copy-start) | copy-done | bytes 262168
  38.3 0.0 copy-start.1
  38.3 0.6 %copy-done.1 = bf16[128,256]{1,0:T(8,128)(2,1)} copy-done((bf16[128,256]{1,0:T(8,128)(2,1)}, bf16[128,256]{1,0:T(8,128)(2,1)S(1)}, u32[]{:S(2)}) %copy-start.1) | copy-done | bytes 65560
  38.9 0.0 copy-start.2
  38.9 0.6 %copy-done.2 = bf16[128,256]{1,0:T(8,128)(2,1)} copy-done((bf16[128,256]{1,0:T(8,128)(2,1)}, bf16[128,256]{1,0:T(8,128)(2,1)S(1)}, u32[]{:S(2)}) %copy-start.2) | copy-done | bytes 65560
  39.5 1.8 %shard_map.95 = (bf16[128,256]{1,0:T(8,128)(2,1)}, bf16[128,256]{1,0:T(8,128)(2,1)}, f32[256,256]{1,0:T(8,128)}) custom-call(bf16[128,256]{1,0:T(8,128)(2,1)} %copy-done.1, bf16[128,256]{1,0:T(8,128)(2,1)} %copy-done.2, f32[256,256]{1,0:T(8,128)} %copy-done), custom_call_target="tpu_custom_call" | custom-call | tf_op jit(solution)/shard_map/pallas_call | solution.py:380
Async XLA Ops:
  37.6 0.7 %copy-start = (f32[256,256]{1,0:T(8,128)}, f32[256,256]{1,0:T(8,128)S(1)}, u32[]{:S(2)}) copy-start(f32[256,256]{1,0:T(8,128)S(1)} %get-tuple-element.8.refs_2_) | copy-start | bytes 786436
  38.3 0.6 %copy-start.1 = (bf16[128,256]{1,0:T(8,128)(2,1)}, bf16[128,256]{1,0:T(8,128)(2,1)S(1)}, u32[]{:S(2)}) copy-start(bf16[128,256]{1,0:T(8,128)(2,1)S(1)} %get-tuple-element.6.refs_0_) | copy-start | bytes 196612
  38.9 0.6 %copy-start.2 = (bf16[128,256]{1,0:T(8,128)(2,1)}, bf16[128,256]{1,0:T(8,128)(2,1)S(1)}, u32[]{:S(2)}) copy-start(bf16[128,256]{1,0:T(8,128)(2,1)S(1)} %get-tuple-element.7.refs_1_) | copy-start | bytes 196612

commit v5 on v4

--- a/solution.py
+++ b/solution.py
@@ -66,7 +66,7 @@
     act, fgrad, wgrad,
     feat_all, tiles, tiles_t, adj, adj_t, weight, weight_t, upstream,
     part_send, part_recv, cot_all, sib_send, sib_recv, back_send, back_recv,
-    w_send, w_recv, w_mid, w_all,
+    w_send, w_recv, w_mid, w_all, slot_of,
     in_sem, sib_s, sib_r,
     feat_s, feat_r, fwd_s, fwd_r, part_s, part_r, cot_s, cot_r,
     pair_s, pair_r, back_s, back_r, w1_s, w1_r, w2_s, w2_r, w3_s, w3_r,
@@ -122,52 +122,53 @@
         barrier, inc=1, device_id=(row_peer(k), j), device_id_type=MESH))
     repeat(1, n_col, lambda k: pl.semaphore_signal(
         barrier, inc=1, device_id=(i, col_peer(k)), device_id_type=MESH))
-    pl.semaphore_wait(barrier, n_row + n_col - 2)
-
-    def feat_copy(h, k, owner):
-        return to_row(feat_in.at[:, strip(h)], feat_all.at[h, block(owner, nodes)],
-                      feat_s.at[h, k], feat_r.at[h, k], mate(k))
-
-    def sib_copy(h, owner):
-        return to_row(feat_in.at[:, strip(h)], feat_all.at[h, block(owner, nodes)],
-                      sib_s.at[h], sib_r.at[h], sibling)
-
-    def pass_copy(h, k, owner):
-        place = feat_all.at[h, block(owner, nodes)]
-        return to_row(place, place, fwd_s.at[h, k], fwd_r.at[h, k], sibling)
-
-    for h in range(PARTS):
-        far_first(n_chip, lambda k: feat_copy(h, k, i).start())
-        sib_copy(h, i).start()
-
-    loads[0].wait()
-    tiles[slots] = jnp.zeros((tile, tile), BF16)
-    tiles_t[slots] = jnp.zeros((tile, tile), BF16)
-
-    def flip(s):
-        tiles_t[s] = tiles[s].T
-
-    repeat(0, slots, flip)
     count = count_ref[0, 0]
 
-    def place_row(r):
-        def place(c):
+    def find_row(r):
+        def find(c):
             slot = jnp.int32(slots)
             for s in range(slots):
                 hit = (rows_ref[0, 0, s] == r) & (cols_ref[0, 0, s] == c) & (s < count)
                 slot = jnp.where(hit, jnp.int32(s), slot)
-            adj[block(r, tile), block(c, tile)] = tiles[slot]
-            adj_t[block(c, tile), block(r, tile)] = tiles_t[slot]
+            slot_of[r * col_tiles + c] = slot
+
+        repeat(0, col_tiles, find)
+
+    repeat(0, row_tiles, find_row)
+    tiles[slots] = jnp.zeros((tile, tile), BF16)
+    tiles_t[slots] = jnp.zeros((tile, tile), BF16)
+    pl.semaphore_wait(barrier, n_row + n_col - 2)
+
+    def feat_copy(h, k, owner):
+        return to_row(feat_in.at[:, strip(h)], feat_all.at[h, block(owner, nodes)],
+                      feat_s.at[h, k], feat_r.at[h, k], mate(k))
+
+    def sib_copy(h, owner):
+        return to_row(feat_in.at[:, strip(h)], feat_all.at[h, block(owner, nodes)],
+                      sib_s.at[h], sib_r.at[h], sibling)
+
+    def pass_copy(h, k, owner):
+        place = feat_all.at[h, block(owner, nodes)]
+        return to_row(place, place, fwd_s.at[h, k], fwd_r.at[h, k], sibling)
+
+    for h in range(PARTS):
+        far_first(n_chip, lambda k: feat_copy(h, k, i).start())
+        sib_copy(h, i).start()
+
+    loads[0].wait()
+
+    def place_row(r):
+        def place(c):
+            adj[block(r, tile), block(c, tile)] = tiles[slot_of[r * col_tiles + c]]
 
         repeat(0, col_tiles, place)
 
     repeat(0, row_tiles, place_row)
-    for load in loads[1:]:
+    for load in loads[3:]:
         load.wait()
-    weight_t[...] = weight[...].T
 
     def part_copy(h, k):
-        return to_col(part_send.at[h, k], part_recv.at[h, k],
+        return to_col(part_send.at[h, block(col_peer(k), nodes)], part_recv.at[h, k],
                       part_s.at[h, k], part_r.at[h, k], col_peer(k))
 
     for h in range(PARTS):
@@ -180,13 +181,36 @@
         sib_copy(h, sibling).wait_recv()
         far_first(n_chip, lambda k: pass_copy(h, k, mate(k) + sibling - i).wait_recv())
 
-        def forward(k):
-            rows = block(col_peer(k), nodes)
-            part_send[h, k] = dot(adj[rows, :], feat_all[h]).astype(BF16)
-            part_copy(h, k).start()
-
-        far_first(n_col, forward)
-        part_recv[h, 0] = dot(adj[block(j, nodes), :], feat_all[h]).astype(BF16)
+        part_send[h] = dot(adj[...], feat_all[h]).astype(BF16)
+        far_first(n_col, lambda k: part_copy(h, k).start())
+        part_recv[h, 0] = part_send[h, block(j, nodes), :]
+
+    def flip(s):
+        tiles_t[s] = tiles[s].T
+
+    repeat(0, slots, flip)
+    per = nodes // tile
+
+    def place_back(r):
+        def place(c):
+            rank = c // per
+            spot = ((rank % 2) * n_chip + rank // 2) * per + c % per
+            adj_t[block(spot, tile), block(r, tile)] = tiles_t[slot_of[r * col_tiles + c]]
+
+        repeat(0, col_tiles, place)
+
+    repeat(0, row_tiles, place_back)
+    loads[1].wait()
+    loads[2].wait()
+    weight_t[...] = weight[...].T
+    for h in range(PARTS):
+
+        def feat_sent(k):
+            feat_copy(h, k, i).wait_send()
+            pass_copy(h, k, mate(k)).wait_send()
+
+        sib_copy(h, i).wait_send()
+        repeat(1, n_chip, feat_sent)
 
     gathered = []
     preact = jnp.zeros((nodes, width), F32)
@@ -222,65 +246,60 @@
 
     far_first(n_row, lambda k: w1_copy(k).start())
     w_recv[0] = w_send[block(i, piece), :]
-
-    def pair_copy(h, k):
-        return to_row(sib_send.at[h, k], sib_recv.at[h, k],
-                      pair_s.at[h, k], pair_r.at[h, k], sibling)
-
-    def back_copy(h, k):
-        return to_row(back_send.at[h, k], back_recv.at[h, k],
-                      back_s.at[h, k], back_r.at[h, k], mate(k))
-
-    def back_dot(h, owner):
-        return dot(adj_t[block(owner, nodes), :], cot_all[h])
-
-    own = []
-    for h in range(PARTS):
-        far_first(n_col, lambda k: cot_copy(h, k, col_peer(k)).wait_recv())
-
-        def to_sibling(k):
-            sib_send[h, k] = back_dot(h, mate(k) + sibling - i).astype(BF16)
-            pair_copy(h, k).start()
-
-        def to_owner(k):
-            mine = back_dot(h, mate(k))
-            pair_copy(h, k).wait_recv()
-            back_send[h, k] = (mine + sib_recv[h, k].astype(F32)).astype(BF16)
-            back_copy(h, k).start()
-
-        far_first(n_chip, to_sibling)
-        to_sibling(0)
-        far_first(n_chip, to_owner)
-        mine = back_dot(h, i)
-        pair_copy(h, 0).wait_recv()
-        own.append(mine + sib_recv[h, 0].astype(F32))
-
-    far_first(n_row, lambda k: w1_copy(k).wait_recv())
-    summed = w_recv[0].astype(F32)
-    for k in range(1, n_row):
-        summed = summed + w_recv[k].astype(F32)
-    w_mid[j] = summed.astype(BF16)
+    for h in range(PARTS):
+        repeat(1, n_col, lambda k: part_copy(h, k).wait_send())
 
     def w2_copy(k, owner):
         return to_col(w_mid.at[owner], w_mid.at[owner], w2_s.at[k], w2_r.at[k], col_peer(k))
-
-    far_first(n_col, lambda k: w2_copy(k, j).start())
-    far_first(n_col, lambda k: w2_copy(k, col_peer(k)).wait_recv())
-    summed = w_mid[0].astype(F32)
-    for k in range(1, n_col):
-        summed = summed + w_mid[k].astype(F32)
-    w_all[block(i, piece), :] = summed.astype(BF16)
 
     def w3_copy(k, owner):
         place = w_all.at[block(owner, piece)]
         return to_row(place, place, w3_s.at[k], w3_r.at[k], row_peer(k))
 
-    far_first(n_row, lambda k: w3_copy(k, i).start())
+    def sum_over_row():
+        far_first(n_row, lambda k: w1_copy(k).wait_recv())
+        summed = w_recv[0].astype(F32)
+        for k in range(1, n_row):
+            summed = summed + w_recv[k].astype(F32)
+        w_mid[j] = summed.astype(BF16)
+        far_first(n_col, lambda k: w2_copy(k, j).start())
+
+    def sum_over_col():
+        far_first(n_col, lambda k: w2_copy(k, col_peer(k)).wait_recv())
+        summed = w_mid[0].astype(F32)
+        for k in range(1, n_col):
+            summed = summed + w_mid[k].astype(F32)
+        w_all[block(i, piece), :] = summed.astype(BF16)
+        far_first(n_row, lambda k: w3_copy(k, i).start())
+
+    def pair_copy(h):
+        return to_row(sib_send.at[h], sib_recv.at[h], pair_s.at[h], pair_r.at[h], sibling)
+
+    def back_copy(h, k):
+        return to_row(back_send.at[h, block(partner(chip, k, n_chip), nodes)],
+                      back_recv.at[h, k], back_s.at[h, k], back_r.at[h, k], mate(k))
+
+    for h in range(PARTS):
+        far_first(n_col, lambda k: cot_copy(h, k, col_peer(k)).wait_recv())
+        sib_send[h] = dot(adj_t[block(1 - core, n_chip * nodes), :], cot_all[h]).astype(BF16)
+        pair_copy(h).start()
+        mine = dot(adj_t[block(core, n_chip * nodes), :], cot_all[h])
+        pair_copy(h).wait_recv()
+        back_send[h] = (mine + sib_recv[h].astype(F32)).astype(BF16)
+        far_first(n_chip, lambda k: back_copy(h, k).start())
+        if h == 0:
+            sum_over_row()
+    sum_over_col()
+    for h in range(PARTS):
+        pair_copy(h).wait_send()
+        repeat(1, n_col, lambda k: cot_copy(h, k, j).wait_send())
+    repeat(1, n_row, lambda k: w1_copy(k).wait_send())
+    repeat(1, n_col, lambda k: w2_copy(k, j).wait_send())
 
     grad = jnp.zeros((nodes, width), F32)
     for h in range(PARTS):
         far_first(n_chip, lambda k: back_copy(h, k).wait_recv())
-        pulled = own[h]
+        pulled = back_send[h, block(chip, nodes), :].astype(F32)
         for k in range(1, n_chip):
             pulled = pulled + back_recv[h, k].astype(F32)
         grad = grad + dot(pulled.astype(BF16), weight_t[strip(h), :])
@@ -290,28 +309,9 @@
     wgrad[:, pl.ds(0, half)] = w_all[pl.ds(0, width), :].astype(F32)
     wgrad[:, pl.ds(half, half)] = w_all[pl.ds(width, width), :].astype(F32)
 
-    def row_sent(k):
-        w1_copy(k).wait_send()
-        w3_copy(k, i).wait_send()
-
-    repeat(1, n_row, row_sent)
-    repeat(1, n_col, lambda k: w2_copy(k, j).wait_send())
-    for h in range(PARTS):
-
-        def chip_sent(k):
-            feat_copy(h, k, i).wait_send()
-            pass_copy(h, k, mate(k)).wait_send()
-            pair_copy(h, k).wait_send()
-            back_copy(h, k).wait_send()
-
-        def col_sent(k):
-            part_copy(h, k).wait_send()
-            cot_copy(h, k, j).wait_send()
-
-        sib_copy(h, i).wait_send()
-        pair_copy(h, 0).wait_send()
-        repeat(1, n_chip, chip_sent)
-        repeat(1, n_col, col_sent)
+    repeat(1, n_row, lambda k: w3_copy(k, i).wait_send())
+    for h in range(PARTS):
+        repeat(1, n_chip, lambda k: back_copy(h, k).wait_send())
 
 
 def hand_over(*refs):
@@ -357,22 +357,23 @@
             vmem((width, width), BF16),
             vmem((width, width), BF16),
             vmem((nodes, width), BF16),
-            vmem((PARTS, n_col, nodes, lanes), BF16),
+            vmem((PARTS, tall, lanes), BF16),
             vmem((PARTS, n_col, nodes, lanes), BF16),
             vmem((PARTS, tall, lanes), BF16),
-            vmem((PARTS, n_chip, nodes, lanes), BF16),
-            vmem((PARTS, n_chip, nodes, lanes), BF16),
-            vmem((PARTS, n_chip, nodes, lanes), BF16),
+            vmem((PARTS, n_chip * nodes, lanes), BF16),
+            vmem((PARTS, n_chip * nodes, lanes), BF16),
+            vmem((PARTS, n_chip * nodes, lanes), BF16),
             vmem((PARTS, n_chip, nodes, lanes), BF16),
             vmem((2 * width, width // 2), BF16),
             vmem((n_row, piece, width // 2), BF16),
             vmem((n_col, piece, width // 2), BF16),
             vmem((2 * width, width // 2), BF16),
+            pltpu.SMEM(((tall // tile) * (wide // tile),), jnp.int32),
             dma((3 + PARTS,)), dma((PARTS,)), dma((PARTS,)),
         ]
         + [dma((PARTS, n_chip))] * 4
         + [dma((PARTS, n_col))] * 4
-        + [dma((PARTS, n_chip))] * 4
+        + [dma((PARTS,))] * 2 + [dma((PARTS, n_chip))] * 2
         + [dma((n_row,))] * 2 + [dma((n_col,))] * 2 + [dma((n_row,))] * 2,
         compiler_params=pltpu.CompilerParams(
             collective_id=0, has_side_effects=True, vmem_limit_bytes=56 * 1024 * 1024),
@@ -383,7 +384,7 @@
         in_specs=[in_vmem] * 3,
         out_specs=(anywhere,) * 3,
         scratch_shapes=[dma((3,))],
-    )(*results))
+    )(*(pltpu.with_memory_space_constraint(r, pltpu.VMEM) for r in results)))
 
 
 def solution(mesh):

time: 41.5 us -> 36.8 us (0.89)
  Pallas kernels: 38.1 us -> 35.4 us
  local copies, waits for them, and re-layouts: 1.93 us -> 0 us
    unnamed x6 -> x0, local copies, waits for them, and re-layouts: 1.93 us -> none
    pallas_call x1, Pallas kernels: 36.3 us -> 34.6 us  [body(): pl.pallas_call(functools.partial(kernel, n_row, n_col), out_shape=tuple((...]
    pallas_call x1, Pallas kernels: 1.8 us -> 0.77 us  [body(): pl.pallas_call(hand_over, out_shape=shapes, in_specs=[in_vmem] * 3, out_s...]
where the time goes in v5:
time: 36.8 us; the launch traced here: 36.6 us
  Pallas kernels  35.4 us (96%)
  between operations  1.29 us (4%)
    pallas_call x1, Pallas kernels, body(): pl.pallas_call(functools.partial(kernel, n_row, n_col), out_shape=tuple((...  34.6 us
    pallas_call x1, Pallas kernels, body(): pl.pallas_call(hand_over, out_shape=shapes, in_specs=[in_vmem] * 3, out_s...  0.77 us

profile of v5, /device:TPU:0, one launch (start us, length us, event | category | flops | bytes accessed | tf_op | source)
XLA Modules:
  0.0 36.6 jit_solution(10131130413904819593)
XLA Ops:
  1.3 34.6 %shard_map.94 = (bf16[128,256]{1,0:T(8,128)(2,1)S(1)}, bf16[128,256]{1,0:T(8,128)(2,1)S(1)}, f32[256,256]{1,0:T(8,128)S(1)}) custom-call(bf16[128,256]{1,0:T(8,128)(2,1)} %feat_in.1, bf16[8,128,128]{2,1,0:T(8,128)(2,1)} %bitcast.1, s32[1,1,8]{2,1,0:T(1,128)} %rows_ref.1, s32[1,1,8]{2,1,0:T(1,128)} %cols_ref.1, s32[1,1]{1,0:T(1,128)S(6)} %copy.10.count_ref, ...), custom_call_target="tpu_custom_call" | custom-call | tf_op jit(solution)/shard_map/pallas_call | solution.py:346
  35.9 0.8 %shard_map.95 = (bf16[128,256]{1,0:T(8,128)(2,1)}, bf16[128,256]{1,0:T(8,128)(2,1)}, f32[256,256]{1,0:T(8,128)}) custom-call(bf16[128,256]{1,0:T(8,128)(2,1)S(1)} %get-tuple-element.6.refs_0_, bf16[128,256]{1,0:T(8,128)(2,1)S(1)} %get-tuple-element.7.refs_1_, f32[256,256]{1,0:T(8,128)S(1)} %get-tuple-element.8.refs_2_), custom_call_target="tpu_custom_call" | custom-call | tf_op jit(solution)/shard_map/pallas_call | solution.py:381

commit v6 on v5

--- a/solution.py
+++ b/solution.py
@@ -122,21 +122,6 @@
         barrier, inc=1, device_id=(row_peer(k), j), device_id_type=MESH))
     repeat(1, n_col, lambda k: pl.semaphore_signal(
         barrier, inc=1, device_id=(i, col_peer(k)), device_id_type=MESH))
-    count = count_ref[0, 0]
-
-    def find_row(r):
-        def find(c):
-            slot = jnp.int32(slots)
-            for s in range(slots):
-                hit = (rows_ref[0, 0, s] == r) & (cols_ref[0, 0, s] == c) & (s < count)
-                slot = jnp.where(hit, jnp.int32(s), slot)
-            slot_of[r * col_tiles + c] = slot
-
-        repeat(0, col_tiles, find)
-
-    repeat(0, row_tiles, find_row)
-    tiles[slots] = jnp.zeros((tile, tile), BF16)
-    tiles_t[slots] = jnp.zeros((tile, tile), BF16)
     pl.semaphore_wait(barrier, n_row + n_col - 2)
 
     def feat_copy(h, k, owner):
@@ -155,6 +140,21 @@
         far_first(n_chip, lambda k: feat_copy(h, k, i).start())
         sib_copy(h, i).start()
 
+    count = count_ref[0, 0]
+    places = [
+        jnp.where(s < count, rows_ref[0, 0, s] * col_tiles + cols_ref[0, 0, s], -1)
+        for s in range(slots)
+    ]
+
+    def find(spot):
+        slot = jnp.int32(slots)
+        for s, place in enumerate(places):
+            slot = jnp.where(place == spot, jnp.int32(s), slot)
+        slot_of[spot] = slot
+
+    repeat(0, row_tiles, lambda r: repeat(0, col_tiles, lambda c: find(r * col_tiles + c)))
+    tiles[slots] = jnp.zeros((tile, tile), BF16)
+    tiles_t[slots] = jnp.zeros((tile, tile), BF16)
     loads[0].wait()
 
     def place_row(r):
@@ -167,9 +167,15 @@
     for load in loads[3:]:
         load.wait()
 
-    def part_copy(h, k):
-        return to_col(part_send.at[h, block(col_peer(k), nodes)], part_recv.at[h, k],
-                      part_s.at[h, k], part_r.at[h, k], col_peer(k))
+    last = PARTS - 1
+    few = nodes // 2
+    chunks = [(h, 0, nodes) for h in range(last)] + [(last, 0, few), (last, few, few)]
+
+    def part_copy(n, k):
+        h, first, size = chunks[n]
+        rows = pl.ds(pl.multiple_of(col_peer(k) * nodes + first, few), size)
+        return to_col(part_send.at[h, rows], part_recv.at[h, k, pl.ds(first, size)],
+                      part_s.at[n, k], part_r.at[n, k], col_peer(k))
 
     for h in range(PARTS):
 
@@ -182,7 +188,9 @@
         far_first(n_chip, lambda k: pass_copy(h, k, mate(k) + sibling - i).wait_recv())
 
         part_send[h] = dot(adj[...], feat_all[h]).astype(BF16)
-        far_first(n_col, lambda k: part_copy(h, k).start())
+        for n, chunk in enumerate(chunks):
+            if chunk[0] == h:
+                far_first(n_col, lambda k: part_copy(n, k).start())
         part_recv[h, 0] = part_send[h, block(j, nodes), :]
 
     def flip(s):
@@ -212,27 +220,41 @@
         sib_copy(h, i).wait_send()
         repeat(1, n_chip, feat_sent)
 
-    gathered = []
-    preact = jnp.zeros((nodes, width), F32)
-    for h in range(PARTS):
-        far_first(n_col, lambda k: part_copy(h, k).wait_recv())
-        total = part_recv[h, 0].astype(F32)
-        for k in range(1, n_col):
-            total = total + part_recv[h, k].astype(F32)
-        gathered.append(total.astype(BF16))
-        preact = preact + dot(gathered[h], weight[strip(h), :])
-    aggregate = jnp.concatenate(gathered, axis=1)
-    value, slope = gelu_and_slope(preact)
-    cotangent = (upstream[...].astype(F32) * slope).astype(BF16)
-
-    def cot_copy(h, k, owner):
-        place = cot_all.at[h, block(owner, nodes)]
-        return to_col(place, place, cot_s.at[h, k], cot_r.at[h, k], col_peer(k))
-
-    for h in range(PARTS):
-        cot_all[h, block(j, nodes), :] = cotangent[:, h * lanes:(h + 1) * lanes]
-        far_first(n_col, lambda k: cot_copy(h, k, j).start())
-    act[...] = value.astype(BF16)
+    sendings = [(None, 0)] + [(h, few) for h in range(PARTS)]
+
+    def cot_copy(n, k, owner):
+        h, first = sendings[n]
+        rows = pl.ds(pl.multiple_of(owner * nodes + first, few), few)
+        place = cot_all.at[:, rows] if h is None else cot_all.at[h, rows]
+        return to_col(place, place, cot_s.at[n, k], cot_r.at[n, k], col_peer(k))
+
+    aggregates, cotangents = [], []
+    for first in (0, few):
+        rows = pl.ds(first, few)
+        gathered = []
+        preact = jnp.zeros((few, width), F32)
+        for h in range(PARTS):
+            for n, chunk in enumerate(chunks):
+                if chunk[0] == h and (chunk[1] == first):
+                    far_first(n_col, lambda k: part_copy(n, k).wait_recv())
+            total = part_recv[h, 0, rows, :].astype(F32)
+            for k in range(1, n_col):
+                total = total + part_recv[h, k, rows, :].astype(F32)
+            gathered.append(total.astype(BF16))
+            preact = preact + dot(gathered[h], weight[strip(h), :])
+        value, slope = gelu_and_slope(preact)
+        cotangent = (upstream[rows, :].astype(F32) * slope).astype(BF16)
+        for h in range(PARTS):
+            spot = pl.ds(pl.multiple_of(j * nodes + first, few), few)
+            cot_all[h, spot, :] = cotangent[:, h * lanes:(h + 1) * lanes]
+        for n, sending in enumerate(sendings):
+            if sending[1] == first:
+                far_first(n_col, lambda k: cot_copy(n, k, j).start())
+        act[rows, :] = value.astype(BF16)
+        aggregates.append(jnp.concatenate(gathered, axis=1))
+        cotangents.append(cotangent)
+    aggregate = jnp.concatenate(aggregates, axis=0)
+    cotangent = jnp.concatenate(cotangents, axis=0)
 
     term = lax.dot_general(aggregate, cotangent, (((0,), (0,)), ((), ())),
                            preferred_element_type=F32)
@@ -246,8 +268,8 @@
 
     far_first(n_row, lambda k: w1_copy(k).start())
     w_recv[0] = w_send[block(i, piece), :]
-    for h in range(PARTS):
-        repeat(1, n_col, lambda k: part_copy(h, k).wait_send())
+    for n in range(len(chunks)):
+        repeat(1, n_col, lambda k: part_copy(n, k).wait_send())
 
     def w2_copy(k, owner):
         return to_col(w_mid.at[owner], w_mid.at[owner], w2_s.at[k], w2_r.at[k], col_peer(k))
@@ -280,7 +302,8 @@
                       back_recv.at[h, k], back_s.at[h, k], back_r.at[h, k], mate(k))
 
     for h in range(PARTS):
-        far_first(n_col, lambda k: cot_copy(h, k, col_peer(k)).wait_recv())
+        for n in (0, 1) if h == 0 else (h + 1,):
+            far_first(n_col, lambda k: cot_copy(n, k, col_peer(k)).wait_recv())
         sib_send[h] = dot(adj_t[block(1 - core, n_chip * nodes), :], cot_all[h]).astype(BF16)
         pair_copy(h).start()
         mine = dot(adj_t[block(core, n_chip * nodes), :], cot_all[h])
@@ -292,7 +315,8 @@
     sum_over_col()
     for h in range(PARTS):
         pair_copy(h).wait_send()
-        repeat(1, n_col, lambda k: cot_copy(h, k, j).wait_send())
+    for n in range(len(sendings)):
+        repeat(1, n_col, lambda k: cot_copy(n, k, j).wait_send())
     repeat(1, n_row, lambda k: w1_copy(k).wait_send())
     repeat(1, n_col, lambda k: w2_copy(k, j).wait_send())
 
@@ -372,7 +396,7 @@
             dma((3 + PARTS,)), dma((PARTS,)), dma((PARTS,)),
         ]
         + [dma((PARTS, n_chip))] * 4
-        + [dma((PARTS, n_col))] * 4
+        + [dma((PARTS + 1, n_col))] * 4
         + [dma((PARTS,))] * 2 + [dma((PARTS, n_chip))] * 2
         + [dma((n_row,))] * 2 + [dma((n_col,))] * 2 + [dma((n_row,))] * 2,
         compiler_params=pltpu.CompilerParams(

time: 36.8 us -> 37.7 us (1.024)
  Pallas kernels: 35.4 us -> 36.3 us
    pallas_call x1, Pallas kernels: 34.6 us -> 35.5 us  [body(): pl.pallas_call(functools.partial(kernel, n_row, n_col), out_shape=tuple((...]
where the time goes in v6:
time: 37.7 us; the launch traced here: 37.6 us
  Pallas kernels  36.3 us (96%)
  between operations  1.29 us (3%)
    pallas_call x1, Pallas kernels, body(): pl.pallas_call(functools.partial(kernel, n_row, n_col), out_shape=tuple((...  35.5 us
    pallas_call x1, Pallas kernels, body(): pl.pallas_call(hand_over, out_shape=shapes, in_specs=[in_vmem] * 3, out_s...  0.77 us

profile of v6, /device:TPU:0, one launch (start us, length us, event | category | flops | bytes accessed | tf_op | source)
XLA Modules:
  0.0 37.6 jit_solution(3221042631356590251)
XLA Ops:
  1.3 35.5 %shard_map.94 = (bf16[128,256]{1,0:T(8,128)(2,1)S(1)}, bf16[128,256]{1,0:T(8,128)(2,1)S(1)}, f32[256,256]{1,0:T(8,128)S(1)}) custom-call(bf16[128,256]{1,0:T(8,128)(2,1)} %feat_in.1, bf16[8,128,128]{2,1,0:T(8,128)(2,1)} %bitcast.1, s32[1,1,8]{2,1,0:T(1,128)} %rows_ref.1, s32[1,1,8]{2,1,0:T(1,128)} %cols_ref.1, s32[1,1]{1,0:T(1,128)S(6)} %copy.10.count_ref, ...), custom_call_target="tpu_custom_call" | custom-call | tf_op jit(solution)/shard_map/pallas_call | solution.py:370
  36.8 0.8 %shard_map.95 = (bf16[128,256]{1,0:T(8,128)(2,1)}, bf16[128,256]{1,0:T(8,128)(2,1)}, f32[256,256]{1,0:T(8,128)}) custom-call(bf16[128,256]{1,0:T(8,128)(2,1)S(1)} %get-tuple-element.6.refs_0_, bf16[128,256]{1,0:T(8,128)(2,1)S(1)} %get-tuple-element.7.refs_1_, f32[256,256]{1,0:T(8,128)S(1)} %get-tuple-element.8.refs_2_), custom_call_target="tpu_custom_call" | custom-call | tf_op jit(solution)/shard_map/pallas_call | solution.py:405

commit v7 on v5

--- a/solution.py
+++ b/solution.py
@@ -123,18 +123,18 @@
     repeat(1, n_col, lambda k: pl.semaphore_signal(
         barrier, inc=1, device_id=(i, col_peer(k)), device_id_type=MESH))
     count = count_ref[0, 0]
-
-    def find_row(r):
-        def find(c):
-            slot = jnp.int32(slots)
-            for s in range(slots):
-                hit = (rows_ref[0, 0, s] == r) & (cols_ref[0, 0, s] == c) & (s < count)
-                slot = jnp.where(hit, jnp.int32(s), slot)
-            slot_of[r * col_tiles + c] = slot
-
-        repeat(0, col_tiles, find)
-
-    repeat(0, row_tiles, find_row)
+    places = [
+        jnp.where(s < count, rows_ref[0, 0, s] * col_tiles + cols_ref[0, 0, s], -1)
+        for s in range(slots)
+    ]
+
+    def find(spot):
+        slot = jnp.int32(slots)
+        for s, place in enumerate(places):
+            slot = jnp.where(place == spot, jnp.int32(s), slot)
+        slot_of[spot] = slot
+
+    repeat(0, row_tiles, lambda r: repeat(0, col_tiles, lambda c: find(r * col_tiles + c)))
     tiles[slots] = jnp.zeros((tile, tile), BF16)
     tiles_t[slots] = jnp.zeros((tile, tile), BF16)
     pl.semaphore_wait(barrier, n_row + n_col - 2)
@@ -283,6 +283,7 @@
         far_first(n_col, lambda k: cot_copy(h, k, col_peer(k)).wait_recv())
         sib_send[h] = dot(adj_t[block(1 - core, n_chip * nodes), :], cot_all[h]).astype(BF16)
         pair_copy(h).start()
+    for h in range(PARTS):
         mine = dot(adj_t[block(core, n_chip * nodes), :], cot_all[h])
         pair_copy(h).wait_recv()
         back_send[h] = (mine + sib_recv[h].astype(F32)).astype(BF16)

time: 36.8 us -> 37.8 us (1.027)
  Pallas kernels: 35.4 us -> 36.3 us
    pallas_call x1, Pallas kernels: 34.6 us -> 35.5 us  [body(): pl.pallas_call(functools.partial(kernel, n_row, n_col), out_shape=tuple((...]
where the time goes in v7:
time: 37.8 us; the launch traced here: 37.6 us
  Pallas kernels  36.3 us (96%)
  between operations  1.29 us (3%)
    pallas_call x1, Pallas kernels, body(): pl.pallas_call(functools.partial(kernel, n_row, n_col), out_shape=tuple((...  35.5 us
    pallas_call x1, Pallas kernels, body(): pl.pallas_call(hand_over, out_shape=shapes, in_specs=[in_vmem] * 3, out_s...  0.77 us

profile of v7, /device:TPU:0, one launch (start us, length us, event | category | flops | bytes accessed | tf_op | source)
XLA Modules:
  0.0 37.6 jit_solution(15122112208909349979)
XLA Ops:
  1.3 35.5 %shard_map.94 = (bf16[128,256]{1,0:T(8,128)(2,1)S(1)}, bf16[128,256]{1,0:T(8,128)(2,1)S(1)}, f32[256,256]{1,0:T(8,128)S(1)}) custom-call(bf16[128,256]{1,0:T(8,128)(2,1)} %feat_in.1, bf16[8,128,128]{2,1,0:T(8,128)(2,1)} %bitcast.1, s32[1,1,8]{2,1,0:T(1,128)} %rows_ref.1, s32[1,1,8]{2,1,0:T(1,128)} %cols_ref.1, s32[1,1]{1,0:T(1,128)S(6)} %copy.10.count_ref, ...), custom_call_target="tpu_custom_call" | custom-call | tf_op jit(solution)/shard_map/pallas_call | solution.py:347
  36.8 0.8 %shard_map.95 = (bf16[128,256]{1,0:T(8,128)(2,1)}, bf16[128,256]{1,0:T(8,128)(2,1)}, f32[256,256]{1,0:T(8,128)}) custom-call(bf16[128,256]{1,0:T(8,128)(2,1)S(1)} %get-tuple-element.6.refs_0_, bf16[128,256]{1,0:T(8,128)(2,1)S(1)} %get-tuple-element.7.refs_1_, f32[256,256]{1,0:T(8,128)S(1)} %get-tuple-element.8.refs_2_), custom_call_target="tpu_custom_call" | custom-call | tf_op jit(solution)/shard_map/pallas_call | solution.py:382

commit v8 on v6

--- a/solution.py
+++ b/solution.py
@@ -220,12 +220,11 @@
         sib_copy(h, i).wait_send()
         repeat(1, n_chip, feat_sent)
 
-    sendings = [(None, 0)] + [(h, few) for h in range(PARTS)]
+    sendings = [(0, 0, few), (0, few, few)] + [(h, 0, nodes) for h in range(1, PARTS)]
 
     def cot_copy(n, k, owner):
-        h, first = sendings[n]
-        rows = pl.ds(pl.multiple_of(owner * nodes + first, few), few)
-        place = cot_all.at[:, rows] if h is None else cot_all.at[h, rows]
+        h, first, size = sendings[n]
+        place = cot_all.at[h, pl.ds(pl.multiple_of(owner * nodes + first, few), size)]
         return to_col(place, place, cot_s.at[n, k], cot_r.at[n, k], col_peer(k))
 
     aggregates, cotangents = [], []
@@ -247,8 +246,8 @@
         for h in range(PARTS):
             spot = pl.ds(pl.multiple_of(j * nodes + first, few), few)
             cot_all[h, spot, :] = cotangent[:, h * lanes:(h + 1) * lanes]
-        for n, sending in enumerate(sendings):
-            if sending[1] == first:
+        for n in range(len(sendings)):
+            if (n == 0) == (first == 0):
                 far_first(n_col, lambda k: cot_copy(n, k, j).start())
         act[rows, :] = value.astype(BF16)
         aggregates.append(jnp.concatenate(gathered, axis=1))

time: 37.7 us -> 36.7 us (0.973)
  Pallas kernels: 36.3 us -> 35.3 us
    pallas_call x1, Pallas kernels: 35.5 us -> 34.5 us  [body(): pl.pallas_call(functools.partial(kernel, n_row, n_col), out_shape=tuple((...]
where the time goes in v8:
time: 36.7 us; the launch traced here: 36.6 us
  Pallas kernels  35.3 us (96%)
  between operations  1.29 us (4%)
    pallas_call x1, Pallas kernels, body(): pl.pallas_call(functools.partial(kernel, n_row, n_col), out_shape=tuple((...  34.5 us
    pallas_call x1, Pallas kernels, body(): pl.pallas_call(hand_over, out_shape=shapes, in_specs=[in_vmem] * 3, out_s...  0.77 us

profile of v8, /device:TPU:0, one launch (start us, length us, event | category | flops | bytes accessed | tf_op | source)
XLA Modules:
  0.0 36.6 jit_solution(1180947299486111007)
XLA Ops:
  1.3 34.5 %shard_map.94 = (bf16[128,256]{1,0:T(8,128)(2,1)S(1)}, bf16[128,256]{1,0:T(8,128)(2,1)S(1)}, f32[256,256]{1,0:T(8,128)S(1)}) custom-call(bf16[128,256]{1,0:T(8,128)(2,1)} %feat_in.1, bf16[8,128,128]{2,1,0:T(8,128)(2,1)} %bitcast.1, s32[1,1,8]{2,1,0:T(1,128)} %rows_ref.1, s32[1,1,8]{2,1,0:T(1,128)} %cols_ref.1, s32[1,1]{1,0:T(1,128)S(6)} %copy.10.count_ref, ...), custom_call_target="tpu_custom_call" | custom-call | tf_op jit(solution)/shard_map/pallas_call | solution.py:369
  35.8 0.8 %shard_map.95 = (bf16[128,256]{1,0:T(8,128)(2,1)}, bf16[128,256]{1,0:T(8,128)(2,1)}, f32[256,256]{1,0:T(8,128)}) custom-call(bf16[128,256]{1,0:T(8,128)(2,1)S(1)} %get-tuple-element.6.refs_0_, bf16[128,256]{1,0:T(8,128)(2,1)S(1)} %get-tuple-element.7.refs_1_, f32[256,256]{1,0:T(8,128)S(1)} %get-tuple-element.8.refs_2_), custom_call_target="tpu_custom_call" | custom-call | tf_op jit(solution)/shard_map/pallas_call | solution.py:404

commit v9 on v8

--- a/solution.py
+++ b/solution.py
@@ -306,12 +306,13 @@
         sib_send[h] = dot(adj_t[block(1 - core, n_chip * nodes), :], cot_all[h]).astype(BF16)
         pair_copy(h).start()
         mine = dot(adj_t[block(core, n_chip * nodes), :], cot_all[h])
+        if h == 0:
+            sum_over_row()
+        if h == PARTS - 1:
+            sum_over_col()
         pair_copy(h).wait_recv()
         back_send[h] = (mine + sib_recv[h].astype(F32)).astype(BF16)
         far_first(n_chip, lambda k: back_copy(h, k).start())
-        if h == 0:
-            sum_over_row()
-    sum_over_col()
     for h in range(PARTS):
         pair_copy(h).wait_send()
     for n in range(len(sendings)):

time: 36.7 us -> 36.8 us (level)
  no operation moved by 1% of the time
where the time goes in v9:
time: 36.8 us; the launch traced here: 36.6 us
  Pallas kernels  35.4 us (96%)
  between operations  1.29 us (4%)
    pallas_call x1, Pallas kernels, body(): pl.pallas_call(functools.partial(kernel, n_row, n_col), out_shape=tuple((...  34.6 us
    pallas_call x1, Pallas kernels, body(): pl.pallas_call(hand_over, out_shape=shapes, in_specs=[in_vmem] * 3, out_s...  0.77 us

profile of v9, /device:TPU:0, one launch (start us, length us, event | category | flops | bytes accessed | tf_op | source)
XLA Modules:
  0.0 36.6 jit_solution(2054406356352135522)
XLA Ops:
  1.3 34.6 %shard_map.94 = (bf16[128,256]{1,0:T(8,128)(2,1)S(1)}, bf16[128,256]{1,0:T(8,128)(2,1)S(1)}, f32[256,256]{1,0:T(8,128)S(1)}) custom-call(bf16[128,256]{1,0:T(8,128)(2,1)} %feat_in.1, bf16[8,128,128]{2,1,0:T(8,128)(2,1)} %bitcast.1, s32[1,1,8]{2,1,0:T(1,128)} %rows_ref.1, s32[1,1,8]{2,1,0:T(1,128)} %cols_ref.1, s32[1,1]{1,0:T(1,128)S(6)} %copy.10.count_ref, ...), custom_call_target="tpu_custom_call" | custom-call | tf_op jit(solution)/shard_map/pallas_call | solution.py:370
  35.9 0.8 %shard_map.95 = (bf16[128,256]{1,0:T(8,128)(2,1)}, bf16[128,256]{1,0:T(8,128)(2,1)}, f32[256,256]{1,0:T(8,128)}) custom-call(bf16[128,256]{1,0:T(8,128)(2,1)S(1)} %get-tuple-element.6.refs_0_, bf16[128,256]{1,0:T(8,128)(2,1)S(1)} %get-tuple-element.7.refs_1_, f32[256,256]{1,0:T(8,128)S(1)} %get-tuple-element.8.refs_2_), custom_call_target="tpu_custom_call" | custom-call | tf_op jit(solution)/shard_map/pallas_call | solution.py:405
